TPU v7x, 128 devices: a whole 4x4x4 slice. The times are simulated.
128 devices in a mesh: section: 4 (over x_lo, core), tp: 8 (over y, x_hi), src: 4 (over z).
Axes of the slice: x: 4 (x_hi: 2, x_lo: 2; x = x_hi * 2 + x_lo), y: 4, z: 4, core: 2. Of those that a mesh axis runs over, the one named last changes fastest.
Arguments:
- prefill_pool: bfloat16 [4, 4, 8, 16, 4, 8, 16, 256], P('src', 'section', 'tp'), may hold values from -6 to 6
- block_scales: bfloat16 [4, 4, 8, 16, 4, 8, 2], P('src', 'section', 'tp'), may hold values from 0.25 to 2
- block_table: int32 [4, 4, 8, 16], P('src', 'section', 'tp'), may hold values from 0 to 15, each once within a row
- prompt_len: int32 [4, 4], replicated, may hold values from 1 to 2048, 5120 in all within a row
- dest_group: int32 [4, 4, 1], replicated, may hold values from 0 to 3; in each aligned block of 4 rows (0 to 3, 4 to 7, ..., all dimensions but the last counted through in order) at most 2 rows name the same one
- res_len: int32 [4, 8], P('src'), may hold values from 1 to 3072, 13824 in all within a row
- res_cache: bfloat16 [4, 32, 8, 3072, 256], P('section', 'src', 'tp'), may hold values from -6 to 6
- queries: bfloat16 [4, 64, 8, 8, 2048], P('section', 'src', 'tp'), may hold values from -1000 to 1000
- new_kv: bfloat16 [4, 64, 8, 8, 256], P('section', 'src', 'tp'), may hold values from -6 to 6
Outputs:
- attn_out: bfloat16 [4, 64, 8, 8, 2048], P('section', 'src', 'tp')
- arrived_cache: bfloat16 [4, 32, 8, 2048, 256], P('section', 'src', 'tp')
Inputs may be any that keep to these rules, and one draw needn't show every extreme that they name: `dest_group`: at most 2 requests of one prefill group name the same decode group, and in some group exactly 2 do. `block_table`: each prefill device's row is a permutation of its 16 pool blocks. `prompt_len`: each prefill group's lengths sum to (4 + 1) * 1024 and the longest is exactly 2048. `res_len`: each decode group's lengths sum to (8 + 1) * 1536 and the longest is exactly 3072.
All inputs are finite; a program needn't handle non-finite values.
Results may differ from a plain program's by a relative error of at most 0.0066.
Values may be sent and summed in bfloat16 or wider, within the bound.
No kernel may reach another device: no remote copies, remote signals or barrier semaphores. Data moves between devices by JAX's collectives and lax.ppermute only.
A program may use at most 192 MiB of HBM per device.

v0:
```python
import jax
import jax.numpy as jnp
from jax import lax
from jax.sharding import PartitionSpec as P


def attend(query_rows, context, length, fresh_kv):
    row_count, head_count, step_count, full_width = query_rows.shape
    head_dim = context.shape[-1] // 2
    group_size = full_width // head_dim
    flattened = query_rows.reshape(row_count, head_count, step_count * group_size, head_dim)
    score_scale = head_dim ** (-0.5)
    history = (
        jnp.einsum(
            "rhmd,rhtd->rhmt",
            flattened,
            context[..., :head_dim],
            preferred_element_type=jnp.float32,
        )
        * score_scale
    )
    places = jnp.arange(context.shape[2])
    history = jnp.where(
        places[None, None, None, :] < length[:, None, None, None], history, -jnp.inf
    )
    own_scores = (
        jnp.einsum(
            "rhmd,rhpd->rhmp",
            flattened,
            fresh_kv[..., :head_dim],
            preferred_element_type=jnp.float32,
        )
        * score_scale
    )
    position = jnp.arange(step_count * group_size) // group_size
    own_scores = jnp.where(
        jnp.arange(step_count)[None, :] <= position[:, None], own_scores, -jnp.inf
    )
    highest = jnp.maximum(jnp.max(history, axis=-1), jnp.max(own_scores, axis=-1))[..., None]
    history_w = jnp.exp(history - highest)
    own_w = jnp.exp(own_scores - highest)
    denominator = jnp.sum(history_w, axis=-1, keepdims=True) + jnp.sum(
        own_w, axis=-1, keepdims=True
    )
    history_w = (history_w / denominator).astype(jnp.bfloat16)
    own_w = (own_w / denominator).astype(jnp.bfloat16)
    blended = jnp.einsum(
        "rhmt,rhtd->rhmd", history_w, context[..., head_dim:], preferred_element_type=jnp.float32
    )
    blended = blended + jnp.einsum(
        "rhmp,rhpd->rhmd", own_w, fresh_kv[..., head_dim:], preferred_element_type=jnp.float32
    )
    return blended.reshape(row_count, head_count, step_count, full_width).astype(jnp.bfloat16)


def ranking(dest_group):
    chosen = dest_group[..., 0]
    request_count = chosen.shape[1]
    matching = chosen[:, :, None] == chosen[:, None, :]
    earlier = jnp.arange(request_count)[None, :] < jnp.arange(request_count)[:, None]
    return (chosen, jnp.sum(matching & earlier[None], axis=-1))


def pack_rows(selector, code_rows, factor_rows):
    packed = jnp.einsum(
        "sr,rnlhbc->slhnbc", selector, code_rows, preferred_element_type=jnp.float32
    )
    factors = jnp.einsum(
        "sr,rnlhe->slhne", selector, factor_rows, preferred_element_type=jnp.float32
    )
    return (packed.astype(jnp.bfloat16), factors.astype(jnp.bfloat16))


def on_device(
    prefill_pool,
    block_scales,
    block_table,
    prompt_len,
    dest_group,
    res_len,
    res_cache,
    queries,
    new_kv,
):
    src_count = lax.axis_size("src")
    tp_count = lax.axis_size("tp")
    decode_group = lax.axis_index("src")
    pool_rows = prefill_pool[0, 0, 0]
    table_rows = block_table[0, 0, 0]
    requests = prompt_len.shape[1]
    per_rank = table_rows.shape[0] // requests
    layers, kv_heads, block_len, row_width = pool_rows.shape[1:]
    head_dim = row_width // 2
    layer_heads = layers * tp_count
    local_heads = kv_heads // tp_count
    resident = res_cache.shape[1]
    slot_count = queries.shape[1] - resident
    capacity = slot_count // src_count
    chosen, arrival_rank = ranking(dest_group)
    code_rows = jnp.take(pool_rows, table_rows, axis=0).reshape(
        requests, per_rank, layer_heads, local_heads, block_len, row_width
    )
    factor_rows = jnp.take(block_scales[0, 0, 0], table_rows, axis=0).reshape(
        requests, per_rank, layer_heads, local_heads, 2
    )
    all_codes, all_factors = (
        lax.all_gather(code_rows, "src", axis=0, tiled=True),
        lax.all_gather(factor_rows, "src", axis=0, tiled=True),
    )
    target = (jnp.arange(src_count)[:, None] * capacity + arrival_rank).reshape(-1)
    wanted = (chosen == decode_group).reshape(-1)
    selector = ((jnp.arange(slot_count)[:, None] == target[None, :]) & wanted[None, :]).astype(
        jnp.bfloat16
    )
    packed, factors = pack_rows(selector, all_codes, all_factors)
    packed, factors = (
        lax.all_to_all(packed, ("section", "tp"), split_axis=1, concat_axis=3, tiled=True),
        lax.all_to_all(factors, ("section", "tp"), split_axis=1, concat_axis=3, tiled=True),
    )
    total_blocks = layer_heads * per_rank
    positions = total_blocks * block_len
    packed = packed.reshape(slot_count, local_heads, total_blocks, block_len, row_width)
    factors = factors.reshape(slot_count, local_heads, total_blocks, 2)
    slot_target = jnp.arange(src_count)[:, None] * capacity + arrival_rank
    hits = (jnp.arange(slot_count)[:, None, None] == slot_target[None]) & (chosen == decode_group)[
        None
    ]
    slot_len = jnp.sum(jnp.where(hits, prompt_len[None], 0), axis=(1, 2))
    inside = (jnp.arange(positions)[None, :] < slot_len[:, None]).reshape(
        slot_count, 1, total_blocks, block_len, 1
    )
    arrived = jnp.where(inside, packed, jnp.zeros((), packed.dtype))
    halves = arrived.reshape(slot_count, local_heads, total_blocks, block_len, 2, head_dim).astype(
        jnp.float32
    )
    weighting = factors.astype(jnp.float32)[:, :, :, None, :, None]
    context = (
        (halves * weighting)
        .astype(jnp.bfloat16)
        .reshape(slot_count, local_heads, positions, row_width)
    )
    query_rows = queries[0]
    fresh_kv = new_kv[0]
    res_out = attend(query_rows[:resident], res_cache[0], res_len[0], fresh_kv[:resident])
    slot_out = attend(query_rows[resident:], context, slot_len, fresh_kv[resident:])
    attn_out = jnp.concatenate([res_out, slot_out], axis=0)[None]
    arrived_cache = arrived.reshape(slot_count, local_heads, positions, row_width)[None]
    return (attn_out, arrived_cache)


def solution(mesh):
    return jax.shard_map(
        on_device,
        mesh=mesh,
        in_specs=(
            P("src", "section", "tp", None, None, None, None, None),
            P("src", "section", "tp", None, None, None, None),
            P("src", "section", "tp", None),
            P(),
            P(),
            P("src", None),
            P("section", "src", "tp", None, None),
            P("section", "src", "tp", None, None),
            P("section", "src", "tp", None, None),
        ),
        out_specs=(P("section", "src", "tp", None, None), P("section", "src", "tp", None, None)),
        check_vma=False,
    )
```

profile of v0, /device:TPU:0, one launch (start us, length us, event | category | flops | bytes accessed | tf_op | source)
XLA Modules:
  0.0 364.4 jit_solution(12935188570969465995)
XLA Ops:
  7.2 0.7 fusion.38
  7.9 0.5 broadcast.279
  8.4 1.3 reduce.21
  9.7 0.1 squeeze.18
  9.8 5.0 %gather_fusion = bf16[16,4,8,16,256]{4,3,2,1,0:T(8,128)(2,1)} fusion(bf16[16,4,8,16,256]{4,3,2,1,0:T(8,128)(2,1)} %bitcast.108, s32[1024]{0:T(1024)S(1)} %pad_clamp_fusion), kind=kCustom, calls=%fused_computation | custom fusion | bytes 8388672 | tf_op jit(solution)/shard_map/jit(_take)/gather | solution.py:100
  14.8 4.7 %select_bitcast_fusion.1 = bf16[4,4,32,1,16,256]{5,4,3,2,1,0:T(8,128)(2,1)} fusion(bf16[4,4,32,1,16,256]{5,4,2,1,0,3:T(8,128)(2,1)} %bitcast.107, pred[4,4]{1,0:T(4,128)(4,1)S(1)} %compare_and_fusion), kind=kLoop, calls=%fused_computation.29 | loop fusion | flops 2097152 | bytes 8388624 | tf_op jit(solution)/shard_map/jit(_take)/select_n | solution.py:100
  19.6 0.1 copy.64
  19.7 0.6 gather_fusion.1
  20.2 0.1 gather.15
  20.3 0.1 broadcast_select_fusion
  20.5 0.2 convert_reduce_fusion
  20.8 0.1 add.82
  20.9 0.1 eq.78
  21.0 13.2 %all_gather.7 = bf16[16,4,32,1,2]{2,1,4,3,0:T(4,128)(2,1)S(1)} all-gather(bf16[4,4,32,1,2]{2,1,4,3,0:T(4,128)(2,1)S(1)} %copy.65), channel_id=1, replica_groups=mesh['section'=4,'tp'=8,'src'=4] {'src'}, dimensions={0}, use_global_device_ids=true | all-gather | bytes 10240 | tf_op jit(solution)/shard_map/all_gather | solution.py:108
  34.2 0.1 fusion.19
  34.3 0.7 copy.67
  35.0 7.3 %all-to-all-start.1 = ((bf16[8,32,1,4,2]{0,4,3,2,1:T(2,128)(2,1)}), bf16[8,32,1,4,2]{0,4,3,2,1:T(2,128)(2,1)S(1)}, u32[]{:S(2)}, u32[]{:S(2)}) async-start(bf16[8,32,1,4,2]{0,4,3,2,1:T(2,128)(2,1)} %copy.67), calls=%async_computation.1 | async-start | bytes 131072 | tf_op jit(solution)/shard_map/all_to_all | solution.py:118
  42.4 134.0 %all-gather.2.cloned.1.call-done = bf16[16,4,32,1,16,256]{5,4,3,2,1,0:T(8,128)(2,1)} async-done(((bf16[4,4,32,1,16,256]{5,4,3,2,1,0:T(8,128)(2,1)}), bf16[16,4,32,1,16,256]{5,4,3,2,1,0:T(8,128)(2,1)}) %all-gather.2.cloned.1.call-update) | async-done | bytes 16777232 | tf_op jit(solution)/shard_map/all_gather | solution.py:107
  176.3 18.9 %convert_bitcast_fusion = bf16[8,32,1,4,16,256]{5,0,4,1,3,2:T(8,128)(2,1)} fusion(bf16[16,4,32,1,16,256]{5,4,3,2,1,0:T(8,128)(2,1)} %all-gather.2.cloned.1.call-done, s32[16]{0:T(128)S(1)} %add.82, pred[16]{0:T(512)(128)(4,1)S(1)} %eq.78), kind=kOutput, calls=%fused_computation.18 | convolution fusion | flops 138412288 | bytes 25165904 | tf_op jit(solution)/shard_map/sr,rnlhbc->slhnbc/dot_general | solution.py:65
  195.3 7.7 %copy.62 = bf16[8,32,1,4,16,256]{5,0,4,3,2,1:T(8,128)(2,1)} copy(bf16[8,32,1,4,16,256]{5,0,4,1,3,2:T(8,128)(2,1)} %convert_bitcast_fusion) | data formatting | bytes 16777216 | tf_op jit(solution)/shard_map/convert_element_type | solution.py:71
  203.0 7.5 %all-to-all-start = ((bf16[8,32,1,4,16,256]{5,0,4,3,2,1:T(8,128)(2,1)}), bf16[8,32,1,4,16,256]{5,0,4,3,2,1:T(8,128)(2,1)}, u32[]{:S(2)}, u32[]{:S(2)}) async-start(bf16[8,32,1,4,16,256]{5,0,4,3,2,1:T(8,128)(2,1)} %copy.62), calls=%async_computation | async-start | bytes 16777216 | tf_op jit(solution)/shard_map/all_to_all | solution.py:117
  210.7 0.1 reshape.489
  210.8 0.1 reshape.480
  211.0 0.3 fusion.45
  211.3 0.1 iota_compare_fusion
  211.3 4.1 %fusion.3 = (f32[8,128]{1,0:T(8,128)S(1)}, f32[8,128,3072]{2,1,0:T(8,128)S(1)}) fusion(pred[8,3072]{1,0:T(8,128)(4,1)S(1)} %iota_compare_fusion, bf16[8,128,128]{2,1,0:T(8,128)(2,1)S(1)} %reshape.480, bf16[8,1,3072,256]{3,2,0,1:T(8,128)(2,1)} %bitcast.109), kind=kOutput, calls=%fused_computation.9 | convolution fusion | flops 814742528 | bytes 19165184 | tf_op jit(solution)/shard_map/rhmd,rhtd->rhmt/dot_general | solution.py:14
  215.5 2.9 fusion.4
  218.4 6.0 %fusion.9 = f32[8,128,128]{2,1,0:T(8,128)S(1)} fusion(bf16[8,1,3072,256]{3,2,0,1:T(8,128)(2,1)} %bitcast.110, f32[8,128,3072]{2,1,0:T(8,128)S(1)} %get-tuple-element.21, f32[8,128]{1,0:T(8,128)S(1)} %add.76, f32[8,128]{1,0:T(8,128)S(1)} %max.18, pred[8,3072]{1,0:T(8,128)(4,1)S(1)} %iota_compare_fusion), kind=kOutput, calls=%fused_computation.21 | convolution fusion | flops 821035008 | bytes 19431424 | tf_op jit(solution)/shard_map/rhmt,rhtd->rhmd/dot_general | solution.py:47
  224.4 0.3 fusion.15
  224.7 0.1 convert_element_type.105
  224.9 0.1 select_reduce_fusion
  225.0 0.3 fusion.44
  225.2 0.1 iota_compare_fusion.1
  225.3 0.1 copy.68
  225.4 0.1 copy.69
  225.5 0.9 copy.70
  226.4 6.8 %mul.55 = f32[8,128,16,2,128]{4,3,2,1,0:T(2,128)} broadcast(f32[8,128,2]{2,1,0:T(8,128)S(1)} %copy.70), dimensions={0,1,3} | broadcast | bytes 16785408 | tf_op jit(solution)/shard_map/mul | solution.py:138
  233.2 21.6 %mul.56 = f32[8,1,2048,256]{3,2,0,1:T(8,128)} reshape(f32[8,128,16,2,128]{4,3,2,1,0:T(2,128)} %mul.55) | data formatting | bytes 33554432 | tf_op jit(solution)/shard_map/mul | solution.py:138
  254.8 58.9 %all-to-all-done = bf16[8,32,1,4,16,256]{5,0,4,3,2,1:T(8,128)(2,1)} async-done(((bf16[8,32,1,4,16,256]{5,0,4,3,2,1:T(8,128)(2,1)}), bf16[8,32,1,4,16,256]{5,0,4,3,2,1:T(8,128)(2,1)}, u32[]{:S(2)}, u32[]{:S(2)}) %all-to-all-start) | async-done | bytes 8388640 | tf_op jit(solution)/shard_map/all_to_all | solution.py:117
  313.7 8.8 %copy.63 = bf16[8,32,1,4,16,256]{5,4,3,1,0,2:T(8,128)(2,1)} copy(bf16[8,32,1,4,16,256]{5,0,4,3,2,1:T(8,128)(2,1)} %all-to-all-done) | data formatting | bytes 16777216 | tf_op jit(solution)/shard_map/all_to_all | solution.py:117
  322.5 8.8 %multiply_convert_fusion = bf16[8,1,2048,256]{3,2,0,1:T(8,128)(2,1)S(1)} fusion(f32[8,1,2048,256]{3,2,0,1:T(8,128)} %mul.56, bf16[8,32,1,4,16,256]{5,4,3,1,0,2:T(8,128)(2,1)} %copy.63, pred[8,2048]{1,0:T(8,128)(4,1)S(1)} %get-tuple-element.15), kind=kLoop, calls=%fused_computation.5 | loop fusion | flops 16777216 | bytes 33570816 | tf_op jit(solution)/shard_map/convert_element_type | solution.py:139
  331.4 7.8 %bitcast_reduce_fusion = (f32[8,128]{1,0:T(8,128)S(1)}, f32[8,2048,128]{2,1,0:T(8,128)S(1)}) fusion(pred[8,2048]{1,0:T(8,128)(4,1)S(1)} %get-tuple-element.14, bf16[8,128,128]{2,1,0:T(8,128)(2,1)S(1)} %reshape.489, bf16[8,1,2048,256]{3,2,0,1:T(8,128)(2,1)S(1)} %multiply_convert_fusion), kind=kOutput, calls=%fused_computation.12 | convolution fusion | flops 543161344 | bytes 12865536 | tf_op jit(solution)/shard_map/rhmd,rhtd->rhmt/dot_general | solution.py:14
  339.2 2.9 fusion.8
  342.1 6.1 %fusion.12 = f32[8,128,128]{2,1,0:T(8,128)S(1)} fusion(bf16[8,1,2048,256]{3,2,0,1:T(8,128)(2,1)S(1)} %multiply_convert_fusion, f32[8,2048,128]{2,1,0:T(8,128)S(1)} %get-tuple-element.17, f32[8,128]{1,0:T(8,128)S(1)} %add.83, f32[8,128]{1,0:T(8,128)S(1)} %max.19, pred[8,2048]{1,0:T(8,128)(4,1)S(1)} %get-tuple-element.14), kind=kOutput, calls=%fused_computation.26 | convolution fusion | flops 547356672 | bytes 13131776 | tf_op jit(solution)/shard_map/rhmt,rhtd->rhmd/dot_general | solution.py:47
  348.3 0.3 fusion.16
  348.6 0.1 convert_element_type.120
  348.7 8.0 %select_bitcast_fusion = bf16[1,8,1,2048,256]{4,3,2,1,0:T(8,128)(2,1)} fusion(bf16[1,8,1,2048,256]{4,3,1,2,0:T(8,128)(2,1)} %bitcast.106, pred[8,2048]{1,0:T(8,128)(4,1)S(1)} %get-tuple-element.15), kind=kLoop, calls=%fused_computation.15 | loop fusion | flops 4194304 | bytes 16793600
  356.7 0.8 maximum_bitcast_fusion
  (35 shorter events, 0.4 us)
Async XLA Ops:
  7.2 169.2 %all-gather.2.cloned.1.call-start = ((), (), s32[]{:S(2)}) async-start(), calls=%async_computation.2 | async-start | bytes 20971520 | tf_op jit(solution)/shard_map/all_gather | solution.py:107
  14.8 4.7 %copy-start.3 = (bf16[1,1,1,16,4,8,2]{3,6,5,4,2,1,0:T(2,128)(2,1)S(1)}, bf16[1,1,1,16,4,8,2]{3,6,5,4,2,1,0:T(2,128)(2,1)}, u32[]{:S(2)}) copy-start(bf16[1,1,1,16,4,8,2]{3,6,5,4,2,1,0:T(2,128)(2,1)} %param.10) | copy-start | bytes 6148
  14.8 5.7 %copy-start.2 = (s32[4,4,1]{1,2,0:T(1,128)S(1)}, s32[4,4,1]{1,2,0:T(1,128)}, u32[]{:S(2)}) copy-start(s32[4,4,1]{1,2,0:T(1,128)} %param.13) | copy-start | bytes 196
  35.0 167.9 %all-to-all-start.1 = ((bf16[8,32,1,4,2]{0,4,3,2,1:T(2,128)(2,1)}), bf16[8,32,1,4,2]{0,4,3,2,1:T(2,128)(2,1)S(1)}, u32[]{:S(2)}, u32[]{:S(2)}) async-start(bf16[8,32,1,4,2]{0,4,3,2,1:T(2,128)(2,1)} %copy.67), calls=%async_computation.1 | async-start | bytes 131072 | tf_op jit(solution)/shard_map/all_to_all | solution.py:118
  202.9 7.7 %copy-start = (bf16[1,16,1,8,2048]{4,3,2,1,0:T(8,128)(2,1)S(1)}, bf16[1,16,1,8,2048]{4,3,2,1,0:T(8,128)(2,1)}, u32[]{:S(2)}) copy-start(bf16[1,16,1,8,2048]{4,3,2,1,0:T(8,128)(2,1)} %param.16) | copy-start | bytes 1572868
  202.9 8.0 %copy-start.1 = (bf16[1,16,1,8,256]{4,3,2,1,0:T(8,128)(2,1)S(1)}, bf16[1,16,1,8,256]{4,3,2,1,0:T(8,128)(2,1)}, u32[]{:S(2)}) copy-start(bf16[1,16,1,8,256]{4,3,2,1,0:T(8,128)(2,1)} %param.17) | copy-start | bytes 196612
  202.9 8.3 %copy-start.5 = (s32[1,8]{1,0:T(1,128)S(1)}, s32[1,8]{1,0:T(1,128)}, u32[]{:S(2)}) copy-start(s32[1,8]{1,0:T(1,128)} %param.14) | copy-start | bytes 100
  203.0 110.7 %all-to-all-start = ((bf16[8,32,1,4,16,256]{5,0,4,3,2,1:T(8,128)(2,1)}), bf16[8,32,1,4,16,256]{5,0,4,3,2,1:T(8,128)(2,1)}, u32[]{:S(2)}, u32[]{:S(2)}) async-start(bf16[8,32,1,4,16,256]{5,0,4,3,2,1:T(8,128)(2,1)} %copy.62), calls=%async_computation | async-start | bytes 16777216 | tf_op jit(solution)/shard_map/all_to_all | solution.py:117
  218.4 6.5 %copy-start.4 = (s32[4,4]{1,0:T(4,128)S(1)}, s32[4,4]{1,0:T(4,128)}, u32[]{:S(2)}) copy-start(s32[4,4]{1,0:T(4,128)} %param.12) | copy-start | bytes 196
Sparse Core Ops, SparseCore 0:
  19.7 156.6 all-gather.1
where the time goes:
time: 371 us; the launch traced here: 364 us
  waiting for transfers between devices  193 us (52%)
  local copies, waits for them, and re-layouts  53.9 us (15%)
  matrix products  44.2 us (12%)
  other arithmetic  31 us (8%)
  starting transfers between devices  14.9 us (4%)
  between operations  14.4 us (4%)
  blocking collectives  13.2 us (4%)
    all_gather x1, waiting for transfers between devices, on_device(): lax.all_gather(code_rows, 'src', axis=0, tiled=True)  134 us
    all_to_all x1, waiting for transfers between devices, on_device(): lax.all_to_all(packed, ('section', 'tp'), split_axis=1, concat_axis=3, ti...  58.9 us
    mul x2, local copies, waits for them, and re-layouts, on_device(): halves * weighting  28.4 us
    dot_general x1, matrix products, pack_rows(): jnp.einsum('sr,rnlhbc->slhnbc', selector, code_rows, preferred_element_ty...  18.9 us
    all_gather x1, blocking collectives, on_device(): lax.all_gather(factor_rows, 'src', axis=0, tiled=True)  13.2 us
    dot_general x2, matrix products, attend(): jnp.einsum('rhmt,rhtd->rhmd', history_w, context[..., head_dim:], preferr...  12.1 us
    dot_general x2, matrix products, attend(): jnp.einsum('rhmd,rhtd->rhmt', flattened, context[..., :head_dim], preferr...  11.9 us
    unnamed x2, other arithmetic  9.34 us
  transfers between devices with their start and end apart: 3, of which 2 were waited for; matrix products, arithmetic and copies ran while one was open for 20% of the time, Pallas kernels for 0%

commit v1 on v0

v1 whole, which is shorter than its diff:
```python
import functools
import math

import jax
import jax.numpy as jnp
from jax import lax
from jax.experimental import pallas as pl
from jax.experimental.pallas import tpu as pltpu
from jax.sharding import PartitionSpec as P

HEAD = 128
STEPS = 8
GROUP = 16
QUERIES = STEPS * GROUP
TILE = 512
BLOCK = 16
EXPONENT = math.log2(math.e) / math.sqrt(HEAD)
SIZES = (512, 1024, 2048)

KEPT_LEN, KEPT_SLOT, KEPT_REQ = 0, 4, 8
MOVED_LEN, MOVED_SLOT, MOVED_REQ, MOVED_SHIFT = 12, 16, 20, 24
SEND, BRANCH = 28, 32
TABLE = 40


def routes(dest, length):
    count = len(dest)
    same = [[dest[i] == dest[j] for j in range(count)] for i in range(count)]
    one = lambda flag: jnp.where(flag, 1, 0)
    moved, rank = [], []
    for i in range(count):
        flag = jnp.int32(0)
        place = jnp.int32(0)
        for j in range(count):
            if j == i:
                continue
            longer = length[j] >= length[i] if j < i else length[j] > length[i]
            flag = flag + one(jnp.logical_and(same[i][j], longer))
            if j < i:
                place = place + one(same[i][j])
        moved.append(flag > 0)
        rank.append(place)
    free = []
    for plane in range(count):
        named = jnp.int32(0)
        for i in range(count):
            named = named + one(dest[i] == plane)
        free.append(named == 0)
    planes = []
    before = jnp.int32(0)
    for i in range(count):
        choice = jnp.int32(0)
        seen = jnp.int32(0)
        for plane in range(count):
            choice = jnp.where(jnp.logical_and(free[plane], seen == before), plane, choice)
            seen = seen + one(free[plane])
        planes.append(jnp.where(moved[i], choice, dest[i]))
        before = before + one(moved[i])
    return planes, moved, rank


def pack_kernel(me_ref, dest_ref, len_ref, block_ref, pool_ref, out_ref, table_ref, hold, in_sem, out_sem):
    groups, requests = 4, 4
    me = me_ref[0]

    def fetch(n):
        return pltpu.make_async_copy(pool_ref.at[block_ref[n]], hold.at[n], in_sem.at[n])

    for n in range(16):
        fetch(n).start()
    own_planes, _, _ = routes(
        [dest_ref[me * requests + i] for i in range(requests)],
        [len_ref[me * requests + i] for i in range(requests)],
    )

    def place(n):
        rows = pl.ds((n % 4) * BLOCK, BLOCK)
        return pltpu.make_async_copy(hold.at[n], out_ref.at[own_planes[n // 4], :, rows], out_sem.at[n])

    for n in range(16):
        fetch(n).wait()
        place(n).start()

    for n in range(TABLE):
        table_ref[n] = 0
    crowded = jnp.int32(0)
    longest = jnp.int32(0)
    shifts_used = [jnp.int32(0)] * 4
    at_plane = [[jnp.int32(0)] * 4 for _ in range(4)]
    for g in range(groups):
        dest = [dest_ref[g * requests + i] for i in range(requests)]
        length = [len_ref[g * requests + i] for i in range(requests)]
        planes, moved, rank = routes(dest, length)
        for i in range(requests):
            slot = g * 2 + rank[i]
            shift = (dest[i] - planes[i] + 4) & 3
            kept = jnp.logical_and(dest[i] == me, jnp.logical_not(moved[i]))

            @pl.when(kept)
            def _():
                table_ref[KEPT_LEN + g] = length[i]
                table_ref[KEPT_SLOT + g] = slot
                table_ref[KEPT_REQ + g] = g * requests + i

            @pl.when(jnp.logical_and(moved[i], dest[i] == me))
            def _():
                table_ref[MOVED_LEN + g] = length[i]
                table_ref[MOVED_SLOT + g] = slot
                table_ref[MOVED_REQ + g] = g * requests + i
                table_ref[MOVED_SHIFT + g] = shift

            @pl.when(jnp.logical_and(moved[i], planes[i] == me))
            def _():
                table_ref[SEND + shift] = g

            longest = jnp.where(moved[i], jnp.maximum(longest, length[i]), longest)
            for s in range(1, 4):
                hit = jnp.logical_and(moved[i], shift == s)
                shifts_used[s] = jnp.where(hit, 1, shifts_used[s])
                for m in range(4):
                    more = at_plane[m][s] + jnp.where(jnp.logical_and(hit, planes[i] == m), 1, 0)
                    at_plane[m][s] = more
                    crowded = jnp.where(more > 1, 1, crowded)
    kinds = shifts_used[1] + shifts_used[2] + shifts_used[3]
    which = shifts_used[2] + 2 * shifts_used[3]
    size = jnp.int32(0)
    for limit in SIZES[:-1]:
        size = size + jnp.where(longest > limit, 1, 0)
    simple = jnp.logical_and(kinds == 1, crowded == 0)
    table_ref[BRANCH] = jnp.where(simple, 1 + which * len(SIZES) + size, 0)

    for n in range(16):
        place(n).wait()


def pack(me, dest, lengths, blocks, pool):
    smem = pl.BlockSpec(memory_space=pltpu.SMEM)
    hbm = pl.BlockSpec(memory_space=pl.ANY)
    return pl.pallas_call(
        pack_kernel,
        out_shape=(
            jax.ShapeDtypeStruct((4, 32, 4 * BLOCK, 2 * HEAD), jnp.bfloat16),
            jax.ShapeDtypeStruct((TABLE,), jnp.int32),
        ),
        in_specs=[smem, smem, smem, smem, hbm],
        out_specs=(hbm, smem),
        scratch_shapes=[
            pltpu.VMEM((16, 32, BLOCK, 2 * HEAD), jnp.bfloat16),
            pltpu.SemaphoreType.DMA((16,)),
            pltpu.SemaphoreType.DMA((16,)),
        ],
        compiler_params=pltpu.CompilerParams(vmem_limit_bytes=12 << 20),
        cost_estimate=pl.CostEstimate(flops=0, bytes_accessed=8 << 20, transcendentals=0),
        name="pack",
    )(me, dest, lengths, blocks, pool)


def query_rows(query):
    wide = query.astype(jnp.float32)
    return jnp.concatenate([wide[:, q * HEAD : (q + 1) * HEAD] for q in range(GROUP)], axis=0).astype(
        jnp.bfloat16
    )


def against(rows, keys):
    return lax.dot_general(rows, keys, (((1,), (1,)), ((), ())), preferred_element_type=jnp.float32)


def open_row(rows, fresh):
    scores = against(rows, fresh[:, :HEAD])
    step = lax.broadcasted_iota(jnp.int32, scores.shape, 0) & (STEPS - 1)
    key = lax.broadcasted_iota(jnp.int32, scores.shape, 1)
    scores = jnp.where(key <= step, scores, -jnp.inf)
    top = jnp.max(scores, axis=1, keepdims=True)
    weights = jnp.exp2((scores - top) * EXPONENT)
    mass = jnp.sum(weights, axis=1, keepdims=True)
    total = jnp.dot(weights.astype(jnp.bfloat16), fresh[:, HEAD:], preferred_element_type=jnp.float32)
    return top, mass, total


def extend_row(state, rows, keys, values, left):
    top, mass, total = state
    scores = against(rows, keys)
    key = lax.broadcasted_iota(jnp.int32, scores.shape, 1)
    scores = jnp.where(key < left, scores, -jnp.inf)
    higher = jnp.maximum(top, jnp.max(scores, axis=1, keepdims=True))
    fade = jnp.exp2((top - higher) * EXPONENT)
    weights = jnp.exp2((scores - higher) * EXPONENT)
    mass = mass * fade + jnp.sum(weights, axis=1, keepdims=True)
    total = total * fade + jnp.dot(weights.astype(jnp.bfloat16), values, preferred_element_type=jnp.float32)
    return higher, mass, total


def close_row(state):
    _, mass, total = state
    done = total / mass
    return jnp.concatenate([done[q * STEPS : (q + 1) * STEPS] for q in range(GROUP)], axis=1).astype(
        jnp.bfloat16
    )


def resident_kernel(len_ref, table_ref, query_ref, fresh_ref, cache_ref, out_ref, arrived_ref, hold, zeros, in_sem, zero_sem):
    resident, context = cache_ref.shape[0], cache_ref.shape[1]
    tiles = context // TILE
    slots, positions = arrived_ref.shape[0], arrived_ref.shape[1]

    def fetch(r, c):
        part = pl.ds(c * TILE, TILE)
        return pltpu.make_async_copy(cache_ref.at[r, part], hold.at[r, part], in_sem.at[r, c])

    for r in range(resident):
        for c in range(tiles):

            @pl.when(c * TILE < len_ref[r])
            def _():
                fetch(r, c).start()

    def clear(s):
        return pltpu.make_async_copy(zeros, arrived_ref.at[s], zero_sem.at[s])

    zeros[...] = jnp.zeros_like(zeros)
    for s in range(slots):
        clear(s).start()

    def one_row(r, carry):
        rows = query_rows(query_ref[r])
        length = jnp.where(r < resident, len_ref[jnp.minimum(r, resident - 1)], 0)

        def tile(c, state):
            fetch(r, c).wait()
            part = pl.ds(pl.multiple_of(c * TILE, TILE), TILE)
            keys = hold[r, part, :HEAD]
            values = hold[r, part, HEAD:]
            return extend_row(state, rows, keys, values, length - c * TILE)

        state = lax.fori_loop(0, (length + TILE - 1) // TILE, tile, open_row(rows, fresh_ref[r]))
        out_ref[r] = close_row(state)
        return carry

    lax.fori_loop(0, query_ref.shape[0], one_row, 0)
    for s in range(slots):
        clear(s).wait()


def resident(lengths, table, queries, fresh, cache, slots, positions):
    smem = pl.BlockSpec(memory_space=pltpu.SMEM)
    vmem = pl.BlockSpec(memory_space=pltpu.VMEM)
    hbm = pl.BlockSpec(memory_space=pl.ANY)
    rows, context = cache.shape[0], cache.shape[1]
    return pl.pallas_call(
        resident_kernel,
        out_shape=(
            jax.ShapeDtypeStruct(queries.shape, jnp.bfloat16),
            jax.ShapeDtypeStruct((slots, positions, 2 * HEAD), jnp.bfloat16),
        ),
        in_specs=[smem, smem, vmem, vmem, hbm],
        out_specs=(vmem, hbm),
        scratch_shapes=[
            pltpu.VMEM((rows, context, 2 * HEAD), jnp.bfloat16),
            pltpu.VMEM((positions, 2 * HEAD), jnp.bfloat16),
            pltpu.SemaphoreType.DMA((rows, context // TILE)),
            pltpu.SemaphoreType.DMA((slots,)),
        ],
        compiler_params=pltpu.CompilerParams(vmem_limit_bytes=24 << 20),
        cost_estimate=pl.CostEstimate(flops=1 << 31, bytes_accessed=20 << 20, transcendentals=4 << 20),
        name="resident",
    )(lengths, table, queries, fresh, cache)


def slot_kernel(
    first, shared, table_ref, factor_ref, query_ref, fresh_ref, codes_ref, _out, _arrived, out_ref, arrived_ref,
    hold, answer, in_sem, code_sem, answer_sem,
):
    resident = out_ref.shape[0] - query_ref.shape[0]
    tiles = codes_ref.shape[1] // TILE
    groups = 4

    def fetch(g, c):
        part = pl.ds(c * TILE, TILE)
        return pltpu.make_async_copy(
            codes_ref.at[0 if shared else g, part], hold.at[0 if shared else g, part], in_sem.at[0 if shared else g, c]
        )

    def put(g, c):
        part = pl.ds(c * TILE, TILE)
        slot = table_ref[first + 4 + g]
        return pltpu.make_async_copy(
            hold.at[0 if shared else g, part], arrived_ref.at[slot, part], code_sem.at[0 if shared else g, c]
        )

    def reply(g):
        slot = table_ref[first + 4 + g]
        return pltpu.make_async_copy(
            answer.at[0 if shared else g], out_ref.at[resident + slot], answer_sem.at[0 if shared else g]
        )

    for g in range(groups):
        for c in range(tiles):

            @pl.when(c * TILE < table_ref[first + g])
            def _():
                fetch(g, c).start()

    ones = jnp.ones((HEAD, HEAD), jnp.bfloat16)

    def one_slot(g, carry):
        length = table_ref[first + g]
        slot = table_ref[first + 4 + g]
        request = table_ref[first + 8 + g]
        at = 0 if shared else g

        @pl.when(length > 0)
        def _():
            rows = query_rows(query_ref[slot])
            key_factor = factor_ref[pl.ds(2 * request, 1), :]
            value_factor = factor_ref[pl.ds(2 * request + 1, 1), :]

            def tile(c, state):
                fetch(g, c).wait()
                part = pl.ds(pl.multiple_of(c * TILE, TILE), TILE)
                left = length - c * TILE

                @pl.when(left < TILE)
                def _():
                    codes = hold[at, part, :]
                    place = lax.broadcasted_iota(jnp.int32, codes.shape, 0)
                    hold[at, part, :] = jnp.where(place < left, codes.astype(jnp.float32), 0.0).astype(jnp.bfloat16)

                put(g, c).start()
                row = lax.broadcasted_iota(jnp.int32, (TILE, HEAD), 0)
                column = lax.broadcasted_iota(jnp.int32, (TILE, HEAD), 1)
                hit = column == row // BLOCK + c * (TILE // BLOCK)

                def scaled(codes, factor):
                    spread = jnp.where(hit, factor, 0.0).astype(jnp.bfloat16)
                    wide = jnp.dot(spread, ones, preferred_element_type=jnp.float32)
                    return (codes.astype(jnp.float32) * wide).astype(jnp.bfloat16)

                keys = scaled(hold[at, part, :HEAD], key_factor)
                values = scaled(hold[at, part, HEAD:], value_factor)
                return extend_row(state, rows, keys, values, left)

            state = lax.fori_loop(0, (length + TILE - 1) // TILE, tile, open_row(rows, fresh_ref[slot]))
            answer[at] = close_row(state)
            reply(g).start()

        return carry

    lax.fori_loop(0, groups, one_slot, 0)
    for g in range(groups):

        @pl.when(table_ref[first + g] > 0)
        def _():
            reply(g).wait()

        for c in range(tiles):

            @pl.when(c * TILE < table_ref[first + g])
            def _():
                put(g, c).wait()


def fill_slots(first, shared, table, factors, queries, fresh, codes, out, arrived):
    smem = pl.BlockSpec(memory_space=pltpu.SMEM)
    vmem = pl.BlockSpec(memory_space=pltpu.VMEM)
    hbm = pl.BlockSpec(memory_space=pl.ANY)
    slots = arrived.shape[0]
    entries, positions = codes.shape[0], codes.shape[1]
    tail = lambda width: pl.BlockSpec((slots, STEPS, width), lambda n: (1, 0, 0))
    return pl.pallas_call(
        functools.partial(slot_kernel, first, shared),
        grid=(1,),
        out_shape=(
            jax.ShapeDtypeStruct(out.shape, out.dtype),
            jax.ShapeDtypeStruct(arrived.shape, arrived.dtype),
        ),
        in_specs=[smem, vmem, tail(queries.shape[-1]), tail(2 * HEAD), hbm, hbm, hbm],
        out_specs=(hbm, hbm),
        input_output_aliases={5: 0, 6: 1},
        scratch_shapes=[
            pltpu.VMEM((entries, positions, 2 * HEAD), jnp.bfloat16),
            pltpu.VMEM((entries, STEPS, queries.shape[-1]), jnp.bfloat16),
            pltpu.SemaphoreType.DMA((entries, positions // TILE)),
            pltpu.SemaphoreType.DMA((entries, positions // TILE)),
            pltpu.SemaphoreType.DMA((entries,)),
        ],
        compiler_params=pltpu.CompilerParams(vmem_limit_bytes=16 << 20),
        cost_estimate=pl.CostEstimate(flops=1 << 30, bytes_accessed=8 << 20, transcendentals=1 << 20),
        name="moved_slots" if first == MOVED_LEN else "kept_slots",
    )(table, factors, queries, fresh, codes, out, arrived)


def shifted(values, shift):
    return lax.ppermute(values, "src", [(g, (g + shift) % 4) for g in range(4)])


def on_device(
    prefill_pool,
    block_scales,
    block_table,
    prompt_len,
    dest_group,
    res_len,
    res_cache,
    queries,
    new_kv,
):
    everywhere = ("src", "section", "tp")
    me = lax.axis_index("src").astype(jnp.int32).reshape(1)
    layer_head = lax.axis_index(("section", "tp"))
    layers, heads, block_len, width = prefill_pool.shape[4:]
    pool = prefill_pool.reshape(16, layers * heads, block_len, width)
    slots = queries.shape[1] - res_cache.shape[1]
    positions = 32 * 4 * block_len
    query_view, fresh_view = queries[0, :, 0], new_kv[0, :, 0]

    packed, table = pack(me, dest_group.reshape(-1), prompt_len.reshape(-1), block_table.reshape(-1), pool)
    landed = lax.all_to_all(
        packed.reshape(128, 4 * block_len, width), everywhere, split_axis=0, concat_axis=0, tiled=True
    ).reshape(4, positions, width)

    out, arrived = resident(res_len.reshape(-1), table, query_view, fresh_view, res_cache[0, :, 0], slots, positions)

    scales = jnp.take(block_scales.reshape(16, layers * heads, 2), block_table.reshape(-1), axis=0)
    scales = scales.transpose(1, 0, 2).reshape(8, 128)
    scales = lax.all_gather(scales, everywhere, axis=0, tiled=True).reshape(128, 32, 32)
    scales = lax.dynamic_index_in_dim(scales, layer_head, axis=1, keepdims=False)
    factors = scales.reshape(4, 32, 4, 4, 2).transpose(0, 2, 4, 1, 3).reshape(32, 128).astype(jnp.float32)

    def kept(landed, out, arrived):
        return fill_slots(KEPT_LEN, False, table, factors, query_view, fresh_view, landed, out, arrived)

    def moved(shared, codes, out, arrived):
        return fill_slots(MOVED_LEN, shared, table, factors, query_view, fresh_view, codes, out, arrived)

    def general(landed, out, arrived):
        codes = jnp.zeros_like(landed)
        for shift in range(1, 4):
            hit = table[MOVED_SHIFT : MOVED_SHIFT + 4] == shift
            codes = jnp.where(hit[:, None, None], shifted(landed, shift), codes)
        out, arrived = kept(landed, out, arrived)
        return moved(False, codes, out, arrived)

    def direct(shift, size, landed, out, arrived):
        leaving = lax.dynamic_slice(landed, (table[SEND + shift], 0, 0), (1, size, width))
        codes = shifted(leaving, shift)
        out, arrived = kept(landed, out, arrived)
        return moved(True, codes, out, arrived)

    branches = [general] + [
        functools.partial(direct, shift, size) for shift in range(1, 4) for size in SIZES
    ]
    out, arrived = lax.switch(table[BRANCH], branches, landed, out, arrived)
    return out[None, :, None], arrived[None, :, None]


def solution(mesh):
    return jax.shard_map(
        on_device,
        mesh=mesh,
        in_specs=(
            P("src", "section", "tp", None, None, None, None, None),
            P("src", "section", "tp", None, None, None, None),
            P("src", "section", "tp", None),
            P(),
            P(),
            P("src", None),
            P("section", "src", "tp", None, None),
            P("section", "src", "tp", None, None),
            P("section", "src", "tp", None, None),
        ),
        out_specs=(P("section", "src", "tp", None, None), P("section", "src", "tp", None, None)),
        check_vma=False,
    )
```

time: 371 us -> 421 us (1.13); the launches traced: 364 us -> 422 us
  blocking collectives: 13.2 us -> 354 us
  waiting for transfers between devices: 193 us -> 0.01 us
  matrix products: 44.2 us -> 0 us
  local copies, waits for them, and re-layouts: 53.9 us -> 16.1 us
  Pallas kernels: 0 us -> 35.6 us
  other arithmetic: 31 us -> 1.45 us
  between operations: 14.4 us -> 1.46 us
    all_gather x1, blocking collectives: 13.2 us -> 354 us  [on_device(): lax.all_gather(scales, everywhere, axis=0, tiled=True).reshape(128, 32, 32)]
    all_gather x1 -> x0, waiting for transfers between devices: 134 us -> none  [on_device(): lax.all_gather(code_rows, 'src', axis=0, tiled=True)]
    all_to_all x2 -> x1, waiting for transfers between devices: 58.9 us -> 0.01 us  [on_device(): lax.all_to_all(packed.reshape(128, 4 * block_len, width), everywhere, spl...]
    dot_general x10 -> x0, matrix products: 44.2 us -> none  [the longest x1 18.9 us: pack_rows(): jnp.einsum('sr,rnlhbc->slhnbc', selector, code_rows, preferred_element_ty...]
    pallas_call x0 -> x4, Pallas kernels: none -> 35.6 us  [the longest x1 20.5 us: resident(): pl.pallas_call(resident_kernel, out_shape=(jax.ShapeDtypeStruct(queries.s...]
    mul x2 -> x0, local copies, waits for them, and re-layouts: 28.4 us -> none  [on_device(): halves * weighting]
    unnamed x14 -> x21, local copies, waits for them, and re-layouts: 0.63 us -> 10.7 us
    convert_element_type x6 -> x1, local copies, waits for them, and re-layouts: 9.61 us -> 0.32 us  [on_device(): scales.reshape(4, 32, 4, 4, 2).transpose(0, 2, 4, 1, 3).reshape(32, 128)]
  transfers between devices with their start and end apart: 3 -> 2, of which waited for: 2 -> 0; matrix products, arithmetic and copies ran while one was open for 20% -> 1% of each run, Pallas kernels for 0% -> 8%
where the time goes in v1:
time: 421 us; the launch traced here: 422 us
  blocking collectives  354 us (84%)
  Pallas kernels  35.6 us (8%)
  local copies, waits for them, and re-layouts  16.1 us (4%)
  starting transfers between devices  11.8 us (3%)
    all_gather x1, blocking collectives, on_device(): lax.all_gather(scales, everywhere, axis=0, tiled=True).reshape(128, 32, 32)  354 us
    pallas_call x1, Pallas kernels, resident(): pl.pallas_call(resident_kernel, out_shape=(jax.ShapeDtypeStruct(queries.s...  20.5 us
    pallas_call x2, Pallas kernels, fill_slots(): pl.pallas_call(functools.partial(slot_kernel, first, shared), grid=(1,),...  12 us
    all_to_all x1, starting transfers between devices, on_device(): lax.all_to_all(packed.reshape(128, 4 * block_len, width), everywhere, spl...  11.7 us
    unnamed x21, local copies, waits for them, and re-layouts  10.7 us
  transfers between devices with their start and end apart: 2, of which 0 were waited for; matrix products, arithmetic and copies ran while one was open for 1% of the time, Pallas kernels for 8%

profile of v1, /device:TPU:0, one launch (start us, length us, event | category | flops | bytes accessed | tf_op | source)
XLA Modules:
  0.0 422.5 jit_solution(9898248452701085003)
XLA Ops:
  0.6 0.5 broadcast.63
  1.1 1.3 reduce.3
  2.5 0.1 reshape.144.dest_ref
  2.6 0.8 reshape.145.len_ref
  3.3 0.0 copy-start.1
  3.3 2.2 copy-done.1
  5.5 0.0 copy-start.3
  5.5 0.7 copy-done.3
  6.2 3.0 pack.1
  9.2 0.0 copy-start.2
  9.2 2.0 copy-done.2
  11.2 0.0 copy-start.9
  11.2 0.0 copy-start.4
  11.2 0.0 copy-start.5
  11.3 0.0 copy-start.6
  11.3 0.0 copy-start.8
  11.3 11.7 %all-to-all-start = ((bf16[128,64,256]{2,1,0:T(8,128)(2,1)}), bf16[128,64,256]{2,1,0:T(8,128)(2,1)}, u32[]{:S(2)}, u32[]{:S(2)}) async-start(bf16[128,64,256]{2,1,0:T(8,128)(2,1)} %bitcast.64), calls=%async_computation | async-start | bytes 8388608 | tf_op jit(solution)/shard_map/all_to_all | solution.py:418
  23.0 0.0 copy-done.9
  23.0 0.1 copy.65
  23.1 0.0 copy-done.4
  23.1 0.6 gather_fusion
  23.7 0.1 fusion
  23.8 0.2 copy.66
  24.0 0.2 reshape.150
  24.2 353.9 %all_gather.3 = bf16[1024,128]{1,0:T(8,128)(2,1)S(1)} all-gather(bf16[8,128]{1,0:T(8,128)(2,1)S(1)} %reshape.150), channel_id=1, replica_groups=mesh['section'=4,'tp'=8,'src'=4] {'src','section','tp'}, dimensions={0}, use_global_device_ids=true | all-gather | bytes 264192 | tf_op jit(solution)/shard_map/all_gather | solution.py:426
  378.0 0.4 reshape.151
  378.5 0.1 constant_dynamic-slice_fusion.9
  378.5 0.1 copy.67
  378.6 0.1 reshape.152
  378.7 0.6 slice.35
  380.0 0.0 copy-done.5
  380.0 0.0 copy-done.6
  380.0 0.0 copy-done.8
  380.0 0.0 copy-start
  380.0 4.6 %copy-done = bf16[1,8,1,3072,256]{4,3,2,1,0:T(8,128)(2,1)S(1)} copy-done((bf16[1,8,1,3072,256]{4,3,2,1,0:T(8,128)(2,1)S(1)}, bf16[1,8,1,3072,256]{4,3,2,1,0:T(8,128)(2,1)}, u32[]{:S(2)}) %copy-start) | copy-done | bytes 12582936
  384.6 20.5 %resident.1 = (bf16[16,8,2048]{2,1,0:T(8,128)(2,1)S(1)}, bf16[8,2048,256]{2,1,0:T(8,128)(2,1)}) custom-call(s32[8]{0:T(128)S(1)} %bitcast.66, s32[40]{0:T(128)S(1)} %get-tuple-element.308.table_ref, bf16[16,8,2048]{2,1,0:T(8,128)(2,1)S(1)} %bitcast.68, bf16[16,8,256]{2,1,0:T(8,128)(2,1)S(1)} %bitcast.80, bf16[8,3072,256]{2,1,0:T(8,128)(2,1)S(1)} %bitcast.62), custom_call_target="tpu_custom_call" | custom-call | flops 2147483648 | bytes 20971520 | tf_op jit(solution)/shard_map/resident/pallas_call | solution.py:250
  405.1 0.0 all-to-all-done
  405.1 16.6 %conditional.1 = ((bf16[16,8,2048]{2,1,0:T(8,128)(2,1)S(1)}, bf16[8,2048,256]{2,1,0:T(8,128)(2,1)})) conditional(s32[]{:T(128)} %bitcast.22, (bf16[4,4,2,32,4]{3,0,2,4,1:T(4,128)(2,1)S(1)}, s32[40]{0:T(128)S(1)}, bf16[128,64,256]{2,1,0:T(8,128)(2,1)}, bf16[16,8,2048]{2,1,0:T(8,128)(2,1)S(1)}, ...), branch_computations={%region_0.1_spmd, %region_1.2_spmd, %region_2.3_spmd, %region_3.4_... | conditional | flops 2153775104 | bytes 83927208 | solution.py:453
  405.4 0.6 slice.31
  407.9 1.0 constant_dynamic-slice_fusion.6
  408.9 0.1 collective-permute-start.9
  409.0 0.3 copy.75
  409.3 0.3 reshape.162.factor_ref
  409.6 11.3 %kept_slots.17 = (bf16[16,8,2048]{2,1,0:T(8,128)(2,1)S(1)}, bf16[8,2048,256]{2,1,0:T(8,128)(2,1)}) custom-call(s32[40]{0:T(128)S(1)} %get-tuple-element.269.table_ref, f32[32,128]{1,0:T(8,128)S(1)} %reshape.162.factor_ref, bf16[16,8,2048]{2,1,0:T(8,128)(2,1)S(1)} %get-tuple-element.271.query_ref, ...), custom_call_target="tpu_custom_call", output_to_operand_aliasing={{0}: (5, {}), {1}: (6, {})} | custom-call | flops 1073741824 | bytes 8388608 | tf_op jit(solution)/shard_map/cond/branch_7_fun/kept_slots/pallas_call | solution.py:370
  421.0 0.0 collective-permute-done.9.codes_ref
  421.0 0.7 moved_slots.17
  421.7 0.0 copy-start.7
  421.7 0.8 copy-done.7
  (3 shorter events, 0.0 us)
Async XLA Ops:
  3.3 2.2 copy-start.1
  5.5 0.7 copy-start.3
  9.2 2.0 copy-start.2
  11.2 11.7 %copy-start.9 = (bf16[1,1,1,16,4,8,2]{3,6,5,4,2,1,0:T(2,128)(2,1)S(1)}, bf16[1,1,1,16,4,8,2]{3,6,5,4,2,1,0:T(2,128)(2,1)}, u32[]{:S(2)}) copy-start(bf16[1,1,1,16,4,8,2]{3,6,5,4,2,1,0:T(2,128)(2,1)} %param.20) | copy-start | bytes 6148
  11.2 11.8 %copy-start.4 = (s32[1,1,1,16]{3,2,1,0:T(1,128)S(1)}, s32[1,1,1,16]{3,2,1,0:T(1,128)}, u32[]{:S(2)}) copy-start(s32[1,1,1,16]{3,2,1,0:T(1,128)} %param.21) | copy-start | bytes 196
  11.2 368.7 %copy-start.5 = (s32[1,8]{1,0:T(1,128)S(1)}, s32[1,8]{1,0:T(1,128)}, u32[]{:S(2)}) copy-start(s32[1,8]{1,0:T(1,128)} %param.24) | copy-start | bytes 100
  11.3 368.7 %copy-start.6 = (bf16[1,16,1,8,2048]{4,3,2,1,0:T(8,128)(2,1)S(1)}, bf16[1,16,1,8,2048]{4,3,2,1,0:T(8,128)(2,1)}, u32[]{:S(2)}) copy-start(bf16[1,16,1,8,2048]{4,3,2,1,0:T(8,128)(2,1)} %param.26) | copy-start | bytes 1572868
  11.3 368.7 %copy-start.8 = (bf16[1,16,1,8,256]{4,3,2,1,0:T(8,128)(2,1)S(1)}, bf16[1,16,1,8,256]{4,3,2,1,0:T(8,128)(2,1)}, u32[]{:S(2)}) copy-start(bf16[1,16,1,8,256]{4,3,2,1,0:T(8,128)(2,1)} %param.27) | copy-start | bytes 196612
  11.3 393.8 %all-to-all-start = ((bf16[128,64,256]{2,1,0:T(8,128)(2,1)}), bf16[128,64,256]{2,1,0:T(8,128)(2,1)}, u32[]{:S(2)}, u32[]{:S(2)}) async-start(bf16[128,64,256]{2,1,0:T(8,128)(2,1)} %bitcast.64), calls=%async_computation | async-start | bytes 8388608 | tf_op jit(solution)/shard_map/all_to_all | solution.py:418
  380.0 4.6 %copy-start = (bf16[1,8,1,3072,256]{4,3,2,1,0:T(8,128)(2,1)S(1)}, bf16[1,8,1,3072,256]{4,3,2,1,0:T(8,128)(2,1)}, u32[]{:S(2)}) copy-start(bf16[1,8,1,3072,256]{4,3,2,1,0:T(8,128)(2,1)} %param.25) | copy-start | bytes 37748740
  408.9 12.1 %collective-permute-start.9 = (bf16[1,512,256]{2,1,0:T(8,128)(2,1)S(1)}, bf16[1,512,256]{2,1,0:T(8,128)(2,1)S(1)}, u32[]{:S(2)}, u32[]{:S(2)}) collective-permute-start(bf16[1,512,256]{2,1,0:T(8,128)(2,1)S(1)} %constant_dynamic-slice_fusion.6), channel_id=1, source_target_pairs={{0,3},{1,0},{2,1},{3,2},{4,7},{5,4},{6,5},{7,6},{8,11},{9,8},{10,9... | collective-permute-start | bytes 786440 | tf_op jit(solution)/shard_map/cond/branch_7_fun/ppermute | solution.py:394
  421.7 0.8 copy-start.7

commit v2 on v1

--- a/solution.py
+++ b/solution.py
@@ -16,11 +16,12 @@
 BLOCK = 16
 EXPONENT = math.log2(math.e) / math.sqrt(HEAD)
 SIZES = (512, 1024, 2048)
+VMEM = 63_200_000
 
 KEPT_LEN, KEPT_SLOT, KEPT_REQ = 0, 4, 8
 MOVED_LEN, MOVED_SLOT, MOVED_REQ, MOVED_SHIFT = 12, 16, 20, 24
-SEND, BRANCH = 28, 32
-TABLE = 40
+SEND, BRANCH, POOL = 28, 32, 40
+TABLE = 56
 
 
 def routes(dest, length):
@@ -64,13 +65,13 @@
     me = me_ref[0]
 
     def fetch(n):
-        return pltpu.make_async_copy(pool_ref.at[block_ref[n]], hold.at[n], in_sem.at[n])
+        return pltpu.make_async_copy(pool_ref.at[block_ref[0, 0, 0, n]], hold.at[n], in_sem.at[n])
 
     for n in range(16):
         fetch(n).start()
     own_planes, _, _ = routes(
-        [dest_ref[me * requests + i] for i in range(requests)],
-        [len_ref[me * requests + i] for i in range(requests)],
+        [dest_ref[me, 0, i] for i in range(requests)],
+        [len_ref[me, i] for i in range(requests)],
     )
 
     def place(n):
@@ -81,15 +82,17 @@
         fetch(n).wait()
         place(n).start()
 
-    for n in range(TABLE):
+    for n in range(POOL):
         table_ref[n] = 0
+    for n in range(16):
+        table_ref[POOL + n] = block_ref[0, 0, 0, n]
     crowded = jnp.int32(0)
     longest = jnp.int32(0)
     shifts_used = [jnp.int32(0)] * 4
     at_plane = [[jnp.int32(0)] * 4 for _ in range(4)]
     for g in range(groups):
-        dest = [dest_ref[g * requests + i] for i in range(requests)]
-        length = [len_ref[g * requests + i] for i in range(requests)]
+        dest = [dest_ref[g, 0, i] for i in range(requests)]
+        length = [len_ref[g, i] for i in range(requests)]
         planes, moved, rank = routes(dest, length)
         for i in range(requests):
             slot = g * 2 + rank[i]
@@ -135,7 +138,7 @@
 
 def pack(me, dest, lengths, blocks, pool):
     smem = pl.BlockSpec(memory_space=pltpu.SMEM)
-    hbm = pl.BlockSpec(memory_space=pl.ANY)
+    hbm = pl.BlockSpec(memory_space=pltpu.HBM)
     return pl.pallas_call(
         pack_kernel,
         out_shape=(
@@ -149,7 +152,7 @@
             pltpu.SemaphoreType.DMA((16,)),
             pltpu.SemaphoreType.DMA((16,)),
         ],
-        compiler_params=pltpu.CompilerParams(vmem_limit_bytes=12 << 20),
+        compiler_params=pltpu.CompilerParams(vmem_limit_bytes=VMEM),
         cost_estimate=pl.CostEstimate(flops=0, bytes_accessed=8 << 20, transcendentals=0),
         name="pack",
     )(me, dest, lengths, blocks, pool)
@@ -199,7 +202,7 @@
     )
 
 
-def resident_kernel(len_ref, table_ref, query_ref, fresh_ref, cache_ref, out_ref, arrived_ref, hold, zeros, in_sem, zero_sem):
+def resident_kernel(len_ref, table_ref, query_ref, fresh_ref, cache_ref, out_ref, arrived_ref, pool_ref, hold, zeros, in_sem, zero_sem):
     resident, context = cache_ref.shape[0], cache_ref.shape[1]
     tiles = context // TILE
     slots, positions = arrived_ref.shape[0], arrived_ref.shape[1]
@@ -211,20 +214,22 @@
     for r in range(resident):
         for c in range(tiles):
 
-            @pl.when(c * TILE < len_ref[r])
+            @pl.when(c * TILE < len_ref[0, r])
             def _():
                 fetch(r, c).start()
 
     def clear(s):
         return pltpu.make_async_copy(zeros, arrived_ref.at[s], zero_sem.at[s])
 
+    for n in range(16):
+        pool_ref[n] = table_ref[POOL + n]
     zeros[...] = jnp.zeros_like(zeros)
     for s in range(slots):
         clear(s).start()
 
     def one_row(r, carry):
         rows = query_rows(query_ref[r])
-        length = jnp.where(r < resident, len_ref[jnp.minimum(r, resident - 1)], 0)
+        length = jnp.where(r < resident, len_ref[0, jnp.minimum(r, resident - 1)], 0)
 
         def tile(c, state):
             fetch(r, c).wait()
@@ -245,23 +250,24 @@
 def resident(lengths, table, queries, fresh, cache, slots, positions):
     smem = pl.BlockSpec(memory_space=pltpu.SMEM)
     vmem = pl.BlockSpec(memory_space=pltpu.VMEM)
-    hbm = pl.BlockSpec(memory_space=pl.ANY)
+    hbm = pl.BlockSpec(memory_space=pltpu.HBM)
     rows, context = cache.shape[0], cache.shape[1]
     return pl.pallas_call(
         resident_kernel,
         out_shape=(
             jax.ShapeDtypeStruct(queries.shape, jnp.bfloat16),
             jax.ShapeDtypeStruct((slots, positions, 2 * HEAD), jnp.bfloat16),
+            jax.ShapeDtypeStruct((16,), jnp.int32),
         ),
         in_specs=[smem, smem, vmem, vmem, hbm],
-        out_specs=(vmem, hbm),
+        out_specs=(vmem, hbm, smem),
         scratch_shapes=[
             pltpu.VMEM((rows, context, 2 * HEAD), jnp.bfloat16),
             pltpu.VMEM((positions, 2 * HEAD), jnp.bfloat16),
             pltpu.SemaphoreType.DMA((rows, context // TILE)),
             pltpu.SemaphoreType.DMA((slots,)),
         ],
-        compiler_params=pltpu.CompilerParams(vmem_limit_bytes=24 << 20),
+        compiler_params=pltpu.CompilerParams(vmem_limit_bytes=VMEM),
         cost_estimate=pl.CostEstimate(flops=1 << 31, bytes_accessed=20 << 20, transcendentals=4 << 20),
         name="resident",
     )(lengths, table, queries, fresh, cache)
@@ -272,11 +278,12 @@
     hold, answer, in_sem, code_sem, answer_sem,
 ):
     resident = out_ref.shape[0] - query_ref.shape[0]
-    tiles = codes_ref.shape[1] // TILE
+    positions = codes_ref.shape[1]
+    tiles = pl.cdiv(positions, TILE)
     groups = 4
 
     def fetch(g, c):
-        part = pl.ds(c * TILE, TILE)
+        part = pl.ds(c * TILE, min(TILE, positions - c * TILE))
         return pltpu.make_async_copy(
             codes_ref.at[0 if shared else g, part], hold.at[0 if shared else g, part], in_sem.at[0 if shared else g, c]
         )
@@ -316,7 +323,12 @@
             value_factor = factor_ref[pl.ds(2 * request + 1, 1), :]
 
             def tile(c, state):
-                fetch(g, c).wait()
+                for n in range(tiles):
+
+                    @pl.when(c == n)
+                    def _():
+                        fetch(g, n).wait()
+
                 part = pl.ds(pl.multiple_of(c * TILE, TILE), TILE)
                 left = length - c * TILE
 
@@ -363,9 +375,9 @@
 def fill_slots(first, shared, table, factors, queries, fresh, codes, out, arrived):
     smem = pl.BlockSpec(memory_space=pltpu.SMEM)
     vmem = pl.BlockSpec(memory_space=pltpu.VMEM)
-    hbm = pl.BlockSpec(memory_space=pl.ANY)
+    hbm = pl.BlockSpec(memory_space=pltpu.HBM)
     slots = arrived.shape[0]
-    entries, positions = codes.shape[0], codes.shape[1]
+    entries, tiles = codes.shape[0], pl.cdiv(codes.shape[1], TILE)
     tail = lambda width: pl.BlockSpec((slots, STEPS, width), lambda n: (1, 0, 0))
     return pl.pallas_call(
         functools.partial(slot_kernel, first, shared),
@@ -378,16 +390,35 @@
         out_specs=(hbm, hbm),
         input_output_aliases={5: 0, 6: 1},
         scratch_shapes=[
-            pltpu.VMEM((entries, positions, 2 * HEAD), jnp.bfloat16),
+            pltpu.VMEM((entries, tiles * TILE, 2 * HEAD), jnp.bfloat16),
             pltpu.VMEM((entries, STEPS, queries.shape[-1]), jnp.bfloat16),
-            pltpu.SemaphoreType.DMA((entries, positions // TILE)),
-            pltpu.SemaphoreType.DMA((entries, positions // TILE)),
+            pltpu.SemaphoreType.DMA((entries, tiles)),
+            pltpu.SemaphoreType.DMA((entries, tiles)),
             pltpu.SemaphoreType.DMA((entries,)),
         ],
-        compiler_params=pltpu.CompilerParams(vmem_limit_bytes=16 << 20),
+        compiler_params=pltpu.CompilerParams(vmem_limit_bytes=VMEM),
         cost_estimate=pl.CostEstimate(flops=1 << 30, bytes_accessed=8 << 20, transcendentals=1 << 20),
         name="moved_slots" if first == MOVED_LEN else "kept_slots",
     )(table, factors, queries, fresh, codes, out, arrived)
+
+
+def leave_kernel(shift, table_ref, codes_ref, out_ref, sem):
+    rows = pl.ds(0, out_ref.shape[0])
+    copy = pltpu.make_async_copy(codes_ref.at[table_ref[SEND + shift], rows], out_ref, sem)
+    copy.start()
+    copy.wait()
+
+
+def leave(shift, size, table, codes):
+    return pl.pallas_call(
+        functools.partial(leave_kernel, shift),
+        out_shape=jax.ShapeDtypeStruct((size, codes.shape[2]), codes.dtype),
+        in_specs=[pl.BlockSpec(memory_space=pltpu.SMEM), pl.BlockSpec(memory_space=pl.ANY)],
+        out_specs=pl.BlockSpec(memory_space=pltpu.VMEM),
+        scratch_shapes=[pltpu.SemaphoreType.DMA],
+        compiler_params=pltpu.CompilerParams(vmem_limit_bytes=VMEM),
+        name="leave",
+    )(table, codes)
 
 
 def shifted(values, shift):
@@ -407,25 +438,25 @@
 ):
     everywhere = ("src", "section", "tp")
     me = lax.axis_index("src").astype(jnp.int32).reshape(1)
-    layer_head = lax.axis_index(("section", "tp"))
     layers, heads, block_len, width = prefill_pool.shape[4:]
     pool = prefill_pool.reshape(16, layers * heads, block_len, width)
     slots = queries.shape[1] - res_cache.shape[1]
     positions = 32 * 4 * block_len
     query_view, fresh_view = queries[0, :, 0], new_kv[0, :, 0]
 
-    packed, table = pack(me, dest_group.reshape(-1), prompt_len.reshape(-1), block_table.reshape(-1), pool)
+    packed, table = pack(me, dest_group.transpose(0, 2, 1), prompt_len, block_table, pool)
     landed = lax.all_to_all(
         packed.reshape(128, 4 * block_len, width), everywhere, split_axis=0, concat_axis=0, tiled=True
     ).reshape(4, positions, width)
 
-    out, arrived = resident(res_len.reshape(-1), table, query_view, fresh_view, res_cache[0, :, 0], slots, positions)
-
-    scales = jnp.take(block_scales.reshape(16, layers * heads, 2), block_table.reshape(-1), axis=0)
-    scales = scales.transpose(1, 0, 2).reshape(8, 128)
-    scales = lax.all_gather(scales, everywhere, axis=0, tiled=True).reshape(128, 32, 32)
-    scales = lax.dynamic_index_in_dim(scales, layer_head, axis=1, keepdims=False)
-    factors = scales.reshape(4, 32, 4, 4, 2).transpose(0, 2, 4, 1, 3).reshape(32, 128).astype(jnp.float32)
+    out, arrived, taken = resident(res_len, table, query_view, fresh_view, res_cache[0, :, 0], slots, positions)
+
+    taken = (jnp.arange(16)[:, None] == taken[None, :]).astype(jnp.bfloat16)
+    scales = block_scales.reshape(16, layers * heads, 2).transpose(1, 2, 0).reshape(64, 16)
+    scales = jnp.dot(scales, taken, preferred_element_type=jnp.float32).astype(jnp.bfloat16)
+    scales = jnp.tile(scales.reshape(1, 32, 32), (4, 1, 1)).reshape(128, 32)
+    scales = lax.all_to_all(scales, everywhere, split_axis=0, concat_axis=0, tiled=True)
+    factors = scales.reshape(4, 32, 2, 4, 4).transpose(0, 3, 2, 1, 4).reshape(32, 128).astype(jnp.float32)
 
     def kept(landed, out, arrived):
         return fill_slots(KEPT_LEN, False, table, factors, query_view, fresh_view, landed, out, arrived)
@@ -442,8 +473,7 @@
         return moved(False, codes, out, arrived)
 
     def direct(shift, size, landed, out, arrived):
-        leaving = lax.dynamic_slice(landed, (table[SEND + shift], 0, 0), (1, size, width))
-        codes = shifted(leaving, shift)
+        codes = shifted(leave(shift, size, table, landed), shift)[None]
         out, arrived = kept(landed, out, arrived)
         return moved(True, codes, out, arrived)
 

time: 421 us -> 128 us (0.30)
  blocking collectives: 354 us -> 20.7 us
  waiting for transfers between devices: 0.01 us -> 51.3 us
  local copies, waits for them, and re-layouts: 16.1 us -> 4.11 us
  Pallas kernels: 35.6 us -> 41.8 us
    all_gather x1 -> x0, blocking collectives: 354 us -> none  [on_device(): lax.all_gather(scales, everywhere, axis=0, tiled=True).reshape(128, 32, 32)]
    all_to_all x1, waiting for transfers between devices: 0.01 us -> 50.8 us  [on_device(): lax.all_to_all(packed.reshape(128, 4 * block_len, width), everywhere, spl...]
    all_to_all x0 -> x1, blocking collectives: none -> 20.7 us  [on_device(): lax.all_to_all(scales, everywhere, split_axis=0, concat_axis=0, tiled=True)]
    unnamed x21 -> x8, local copies, waits for them, and re-layouts: 10.7 us -> 0.81 us
    all_to_all x1, starting transfers between devices: 11.7 us -> 5.82 us  [on_device(): lax.all_to_all(packed.reshape(128, 4 * block_len, width), everywhere, spl...]
  transfers between devices with their start and end apart: 2 -> 2, of which waited for: 0 -> 2; matrix products, arithmetic and copies ran while one was open for 1% -> 2% of each run, Pallas kernels for 8% -> 9%
where the time goes in v2:
time: 128 us
  waiting for transfers between devices  51.3 us (40%)
  Pallas kernels  41.8 us (33%)
  blocking collectives  20.7 us (16%)
  starting transfers between devices  7.62 us (6%)
  local copies, waits for them, and re-layouts  4.11 us (3%)
  between operations  1.39 us (1%)
    all_to_all x1, waiting for transfers between devices, on_device(): lax.all_to_all(packed.reshape(128, 4 * block_len, width), everywhere, spl...  50.8 us
    pallas_call x1, Pallas kernels, resident(): pl.pallas_call(resident_kernel, out_shape=(jax.ShapeDtypeStruct(queries.s...  21.7 us
    all_to_all x1, blocking collectives, on_device(): lax.all_to_all(scales, everywhere, split_axis=0, concat_axis=0, tiled=True)  20.7 us
    pallas_call x2, Pallas kernels, fill_slots(): pl.pallas_call(functools.partial(slot_kernel, first, shared), grid=(1,),...  12.5 us
    all_to_all x1, starting transfers between devices, on_device(): lax.all_to_all(packed.reshape(128, 4 * block_len, width), everywhere, spl...  5.82 us
    pallas_call x1, Pallas kernels, pack(): pl.pallas_call(pack_kernel, out_shape=(jax.ShapeDtypeStruct((4, 32, 4 * B...  5.23 us
  transfers between devices with their start and end apart: 2, of which 2 were waited for; matrix products, arithmetic and copies ran while one was open for 2% of the time, Pallas kernels for 9%

profile of v2, /device:TPU:0, one launch (start us, length us, event | category | flops | bytes accessed | tf_op | source)
XLA Modules:
  0.0 127.8 jit_solution(16192705299311934969)
XLA Ops:
  0.6 0.0 copy-start
  0.6 5.2 %pack.1 = (bf16[4,32,64,256]{3,2,1,0:T(8,128)(2,1)}, s32[56]{0:T(128)S(1)}) custom-call(s32[1]{0:T(128)} %bitcast.19.me_ref, s32[4,1,4]{2,1,0:T(1,128)} %bitcast.111, s32[4,4]{1,0:T(4,128)} %len_ref.2, s32[1,1,1,16]{3,2,1,0:T(1,128)} %block_ref.1, bf16[16,32,16,256]{3,2,1,0:T(8,128)(2,1)} %bitcast.90), custom_call_target="tpu_custom_call" | custom-call | bytes 8388608 | tf_op jit(solution)/shard_map/pack/pallas_call | solution.py:142
  5.9 0.0 copy-start.1
  5.9 0.0 copy-start.3
  5.9 21.7 %resident.1 = (bf16[16,8,2048]{2,1,0:T(8,128)(2,1)S(1)}, bf16[8,2048,256]{2,1,0:T(8,128)(2,1)}, s32[16]{0:T(128)}) custom-call(s32[1,8]{1,0:T(1,128)} %len_ref.3, s32[56]{0:T(128)S(1)} %get-tuple-element.309.table_ref, bf16[16,8,2048]{2,1,0:T(8,128)(2,1)} %bitcast.66, bf16[16,8,256]{2,1,0:T(8,128)(2,1)} %bitcast.78, bf16[8,3072,256]{2,1,0:T(8,128)(2,1)} %bitcast.89), custom_call_target="tpu_custom_call" | custom-call | flops 2147483648 | bytes 20971520 | tf_op jit(solution)/shard_map/resident/pallas_call | solution.py:255
  27.6 0.0 copy-done
  27.6 0.8 fusion
  28.4 0.1 copy.79
  28.5 0.1 tile.7
  28.6 0.1 copy.80
  28.8 0.1 all_to_all.9
  28.9 0.1 copy.81
  29.0 20.7 %all_to_all.14 = bf16[128,1,32]{2,1,0:T(2,128)(2,1)S(1)} all-to-all(bf16[128,1,32]{2,1,0:T(2,128)(2,1)S(1)} %copy.81), channel_id=1, replica_groups=mesh['section'=4,'tp'=8,'src'=4] {'src','section','tp'}, dimensions={0} | all-to-all | bytes 16384 | tf_op jit(solution)/shard_map/all_to_all | solution.py:458
  49.7 5.8 %all-to-all-start.1 = ((bf16[128,64,256]{2,1,0:T(8,128)(2,1)}), bf16[128,64,256]{2,1,0:T(8,128)(2,1)}, u32[]{:S(2)}, u32[]{:S(2)}) async-start(bf16[128,64,256]{2,1,0:T(8,128)(2,1)} %bitcast.91), calls=%async_computation.1 | async-start | bytes 8388608 | tf_op jit(solution)/shard_map/all_to_all | solution.py:448
  55.5 0.6 slice.8
  56.8 0.1 copy.82
  56.8 0.1 reshape.103
  56.9 50.8 %all-to-all-done.1 = bf16[128,64,256]{2,1,0:T(8,128)(2,1)} async-done(((bf16[128,64,256]{2,1,0:T(8,128)(2,1)}), bf16[128,64,256]{2,1,0:T(8,128)(2,1)}, u32[]{:S(2)}, u32[]{:S(2)}) %all-to-all-start.1) | async-done | bytes 4194336 | tf_op jit(solution)/shard_map/all_to_all | solution.py:448
  107.7 0.0 copy-done.1
  107.7 0.0 copy-done.3
  107.7 19.3 %conditional.1 = ((bf16[16,8,2048]{2,1,0:T(8,128)(2,1)S(1)}, bf16[8,2048,256]{2,1,0:T(8,128)(2,1)})) conditional(s32[]{:T(128)} %bitcast.23, (bf16[4,4,2,32,4]{3,0,4,1,2:T(4,128)(2,1)S(1)}, s32[56]{0:T(128)S(1)}, bf16[128,64,256]{2,1,0:T(8,128)(2,1)}, bf16[16,8,2048]{2,1,0:T(8,128)(2,1)S(1)}, ...), branch_computations={%region_0.1_spmd, %region_1.2_spmd, %region_2.3_spmd, %region_3.4_... | conditional | flops 2153775104 | bytes 83927208 | solution.py:483
  107.7 2.4 %leave.13 = bf16[1024,256]{1,0:T(8,128)(2,1)} custom-call(s32[56]{0:T(128)S(1)} %get-tuple-element.247.table_ref, bf16[4,2048,256]{2,1,0:T(8,128)(2,1)} %bitcast.9.codes_ref), custom_call_target="tpu_custom_call" | custom-call | tf_op jit(solution)/shard_map/cond/branch_5_fun/leave/pallas_call | solution.py:413
  110.1 1.8 %collective-permute-start.4 = (bf16[1024,256]{1,0:T(8,128)(2,1)}, bf16[1024,256]{1,0:T(8,128)(2,1)S(1)}, u32[]{:S(2)}, u32[]{:S(2)}) collective-permute-start(bf16[1024,256]{1,0:T(8,128)(2,1)} %leave.13), channel_id=1, source_target_pairs={{0,2},{1,3},{2,0},{3,1},{4,6},{5,7},{6,4},{7,5},{8,10},{9,11},{10,... | collective-permute-start | bytes 1572872 | tf_op jit(solution)/shard_map/cond/branch_5_fun/ppermute | solution.py:425
  111.9 0.3 copy.88
  112.2 0.9 reshape.110.factor_ref
  113.2 11.6 %kept_slots.15 = (bf16[16,8,2048]{2,1,0:T(8,128)(2,1)S(1)}, bf16[8,2048,256]{2,1,0:T(8,128)(2,1)}) custom-call(s32[56]{0:T(128)S(1)} %get-tuple-element.247.table_ref, f32[32,128]{1,0:T(8,128)} %reshape.110.factor_ref, bf16[16,8,2048]{2,1,0:T(8,128)(2,1)S(1)} %get-tuple-element.249.query_ref, ...), custom_call_target="tpu_custom_call", output_to_operand_aliasing={{0}: (5, {}), {1}: (6, {})} | custom-call | flops 1073741824 | bytes 8388608 | tf_op jit(solution)/shard_map/cond/branch_5_fun/kept_slots/pallas_call | solution.py:382
  124.8 0.5 collective-permute-done.4
  125.3 0.0 copy-start.8
  125.4 0.8 copy-done.8
  126.1 0.9 moved_slots.15
  127.1 0.0 copy-start.2
  127.1 0.8 copy-done.2
  (1 shorter events, 0.0 us)
Async XLA Ops:
  0.6 27.0 %copy-start = (bf16[1,1,1,16,4,8,2]{3,6,5,4,2,1,0:T(2,128)(2,1)S(1)}, bf16[1,1,1,16,4,8,2]{3,6,5,4,2,1,0:T(2,128)(2,1)}, u32[]{:S(2)}) copy-start(bf16[1,1,1,16,4,8,2]{3,6,5,4,2,1,0:T(2,128)(2,1)} %param.20) | copy-start | bytes 6148
  5.9 101.9 %copy-start.1 = (bf16[1,16,1,8,2048]{4,3,2,1,0:T(8,128)(2,1)S(1)}, bf16[1,16,1,8,2048]{4,3,2,1,0:T(8,128)(2,1)}, u32[]{:S(2)}) copy-start(bf16[1,16,1,8,2048]{4,3,2,1,0:T(8,128)(2,1)} %param.26) | copy-start | bytes 1572868
  5.9 101.8 %copy-start.3 = (bf16[1,16,1,8,256]{4,3,2,1,0:T(8,128)(2,1)S(1)}, bf16[1,16,1,8,256]{4,3,2,1,0:T(8,128)(2,1)}, u32[]{:S(2)}) copy-start(bf16[1,16,1,8,256]{4,3,2,1,0:T(8,128)(2,1)} %param.27) | copy-start | bytes 196612
  49.7 58.0 %all-to-all-start.1 = ((bf16[128,64,256]{2,1,0:T(8,128)(2,1)}), bf16[128,64,256]{2,1,0:T(8,128)(2,1)}, u32[]{:S(2)}, u32[]{:S(2)}) async-start(bf16[128,64,256]{2,1,0:T(8,128)(2,1)} %bitcast.91), calls=%async_computation.1 | async-start | bytes 8388608 | tf_op jit(solution)/shard_map/all_to_all | solution.py:448
  110.1 15.2 %collective-permute-start.4 = (bf16[1024,256]{1,0:T(8,128)(2,1)}, bf16[1024,256]{1,0:T(8,128)(2,1)S(1)}, u32[]{:S(2)}, u32[]{:S(2)}) collective-permute-start(bf16[1024,256]{1,0:T(8,128)(2,1)} %leave.13), channel_id=1, source_target_pairs={{0,2},{1,3},{2,0},{3,1},{4,6},{5,7},{6,4},{7,5},{8,10},{9,11},{10,... | collective-permute-start | bytes 1572872 | tf_op jit(solution)/shard_map/cond/branch_5_fun/ppermute | solution.py:425
  125.3 0.8 copy-start.8
  127.1 0.8 copy-start.2

commit v3 on v2

--- a/solution.py
+++ b/solution.py
@@ -14,14 +14,18 @@
 QUERIES = STEPS * GROUP
 TILE = 512
 BLOCK = 16
+CHUNK = 4 * BLOCK
+SPAN = TILE // CHUNK
+FACTORS = 2 * CHUNK
+CHUNK_ROWS = 2 * CHUNK + 8
 EXPONENT = math.log2(math.e) / math.sqrt(HEAD)
-SIZES = (512, 1024, 2048)
+SIZES = (512, 1024, 1536, 2048)
 VMEM = 63_200_000
 
-KEPT_LEN, KEPT_SLOT, KEPT_REQ = 0, 4, 8
-MOVED_LEN, MOVED_SLOT, MOVED_REQ, MOVED_SHIFT = 12, 16, 20, 24
-SEND, BRANCH, POOL = 28, 32, 40
-TABLE = 56
+KEPT_LEN, KEPT_SLOT = 0, 4
+MOVED_LEN, MOVED_SLOT, MOVED_SHIFT = 8, 12, 16
+SEND, BRANCH = 20, 24
+TABLE = 32
 
 
 def routes(dest, length):
@@ -60,7 +64,10 @@
     return planes, moved, rank
 
 
-def pack_kernel(me_ref, dest_ref, len_ref, block_ref, pool_ref, out_ref, table_ref, hold, in_sem, out_sem):
+def pack_kernel(
+    me_ref, dest_ref, len_ref, block_ref, scale_ref, pool_ref, out_ref, table_ref,
+    hold, wide, in_sem, key_sem, value_sem, wide_sem,
+):
     groups, requests = 4, 4
     me = me_ref[0]
 
@@ -75,17 +82,38 @@
     )
 
     def place(n):
-        rows = pl.ds((n % 4) * BLOCK, BLOCK)
-        return pltpu.make_async_copy(hold.at[n], out_ref.at[own_planes[n // 4], :, rows], out_sem.at[n])
+        block = (n % 4) * BLOCK
+        keys = out_ref.at[own_planes[n // 4], :, pl.ds(block, BLOCK)]
+        values = out_ref.at[own_planes[n // 4], :, pl.ds(CHUNK + block, BLOCK)]
+        return (
+            pltpu.make_async_copy(hold.at[n, :, :, pl.ds(0, HEAD)], keys, key_sem.at[n]),
+            pltpu.make_async_copy(hold.at[n, :, :, pl.ds(HEAD, HEAD)], values, value_sem.at[n]),
+        )
+
+    def place_factors(i):
+        rows = out_ref.at[own_planes[i], :, pl.ds(FACTORS, 8)]
+        return pltpu.make_async_copy(wide.at[i], rows, wide_sem.at[i])
+
+    scales = scale_ref[...].astype(jnp.float32)
+    block = (lax.broadcasted_iota(jnp.int32, scales.shape, 0) >> 1) & 3
+    entry = lax.broadcasted_iota(jnp.int32, scales.shape, 1)
+    ones = jnp.ones((scales.shape[1], HEAD), jnp.bfloat16)
+    for i in range(requests):
+        wanted = jnp.full(scales.shape, block_ref[0, 0, 0, 4 * i], jnp.int32)
+        for k in range(1, 4):
+            wanted = jnp.where(block == k, block_ref[0, 0, 0, 4 * i + k], wanted)
+        picked = jnp.where(entry == wanted, scales, 0.0).astype(jnp.bfloat16)
+        spread = jnp.dot(picked, ones, preferred_element_type=jnp.float32)
+        wide[i] = spread.reshape(wide.shape[1:]).astype(jnp.bfloat16)
+        place_factors(i).start()
 
     for n in range(16):
         fetch(n).wait()
-        place(n).start()
-
-    for n in range(POOL):
+        for copy in place(n):
+            copy.start()
+
+    for n in range(TABLE):
         table_ref[n] = 0
-    for n in range(16):
-        table_ref[POOL + n] = block_ref[0, 0, 0, n]
     crowded = jnp.int32(0)
     longest = jnp.int32(0)
     shifts_used = [jnp.int32(0)] * 4
@@ -103,13 +131,11 @@
             def _():
                 table_ref[KEPT_LEN + g] = length[i]
                 table_ref[KEPT_SLOT + g] = slot
-                table_ref[KEPT_REQ + g] = g * requests + i
 
             @pl.when(jnp.logical_and(moved[i], dest[i] == me))
             def _():
                 table_ref[MOVED_LEN + g] = length[i]
                 table_ref[MOVED_SLOT + g] = slot
-                table_ref[MOVED_REQ + g] = g * requests + i
                 table_ref[MOVED_SHIFT + g] = shift
 
             @pl.when(jnp.logical_and(moved[i], planes[i] == me))
@@ -133,29 +159,36 @@
     table_ref[BRANCH] = jnp.where(simple, 1 + which * len(SIZES) + size, 0)
 
     for n in range(16):
-        place(n).wait()
-
-
-def pack(me, dest, lengths, blocks, pool):
+        for copy in place(n):
+            copy.wait()
+    for i in range(requests):
+        place_factors(i).wait()
+
+
+def pack(me, dest, lengths, blocks, scales, pool):
     smem = pl.BlockSpec(memory_space=pltpu.SMEM)
+    vmem = pl.BlockSpec(memory_space=pltpu.VMEM)
     hbm = pl.BlockSpec(memory_space=pltpu.HBM)
     return pl.pallas_call(
         pack_kernel,
         out_shape=(
-            jax.ShapeDtypeStruct((4, 32, 4 * BLOCK, 2 * HEAD), jnp.bfloat16),
+            jax.ShapeDtypeStruct((4, 32, CHUNK_ROWS, HEAD), jnp.bfloat16),
             jax.ShapeDtypeStruct((TABLE,), jnp.int32),
         ),
-        in_specs=[smem, smem, smem, smem, hbm],
+        in_specs=[smem, smem, smem, smem, vmem, hbm],
         out_specs=(hbm, smem),
         scratch_shapes=[
             pltpu.VMEM((16, 32, BLOCK, 2 * HEAD), jnp.bfloat16),
+            pltpu.VMEM((4, 32, 8, HEAD), jnp.bfloat16),
             pltpu.SemaphoreType.DMA((16,)),
             pltpu.SemaphoreType.DMA((16,)),
+            pltpu.SemaphoreType.DMA((16,)),
+            pltpu.SemaphoreType.DMA((4,)),
         ],
         compiler_params=pltpu.CompilerParams(vmem_limit_bytes=VMEM),
         cost_estimate=pl.CostEstimate(flops=0, bytes_accessed=8 << 20, transcendentals=0),
         name="pack",
-    )(me, dest, lengths, blocks, pool)
+    )(me, dest, lengths, blocks, scales, pool)
 
 
 def query_rows(query):
@@ -202,10 +235,10 @@
     )
 
 
-def resident_kernel(len_ref, table_ref, query_ref, fresh_ref, cache_ref, out_ref, arrived_ref, pool_ref, hold, zeros, in_sem, zero_sem):
+def resident_kernel(len_ref, table_ref, query_ref, fresh_ref, cache_ref, out_ref, arrived_ref, hold, zeros, in_sem, zero_sem):
     resident, context = cache_ref.shape[0], cache_ref.shape[1]
     tiles = context // TILE
-    slots, positions = arrived_ref.shape[0], arrived_ref.shape[1]
+    slots = arrived_ref.shape[0]
 
     def fetch(r, c):
         part = pl.ds(c * TILE, TILE)
@@ -221,8 +254,6 @@
     def clear(s):
         return pltpu.make_async_copy(zeros, arrived_ref.at[s], zero_sem.at[s])
 
-    for n in range(16):
-        pool_ref[n] = table_ref[POOL + n]
     zeros[...] = jnp.zeros_like(zeros)
     for s in range(slots):
         clear(s).start()
@@ -256,14 +287,13 @@
         resident_kernel,
         out_shape=(
             jax.ShapeDtypeStruct(queries.shape, jnp.bfloat16),
-            jax.ShapeDtypeStruct((slots, positions, 2 * HEAD), jnp.bfloat16),
-            jax.ShapeDtypeStruct((16,), jnp.int32),
+            jax.ShapeDtypeStruct((slots, positions // CHUNK, CHUNK, 2 * HEAD), jnp.bfloat16),
         ),
         in_specs=[smem, smem, vmem, vmem, hbm],
-        out_specs=(vmem, hbm, smem),
+        out_specs=(vmem, hbm),
         scratch_shapes=[
             pltpu.VMEM((rows, context, 2 * HEAD), jnp.bfloat16),
-            pltpu.VMEM((positions, 2 * HEAD), jnp.bfloat16),
+            pltpu.VMEM((positions // CHUNK, CHUNK, 2 * HEAD), jnp.bfloat16),
             pltpu.SemaphoreType.DMA((rows, context // TILE)),
             pltpu.SemaphoreType.DMA((slots,)),
         ],
@@ -274,82 +304,82 @@
 
 
 def slot_kernel(
-    first, shared, table_ref, factor_ref, query_ref, fresh_ref, codes_ref, _out, _arrived, out_ref, arrived_ref,
-    hold, answer, in_sem, code_sem, answer_sem,
+    first, shared, table_ref, query_ref, fresh_ref, codes_ref, _out, _arrived, out_ref, arrived_ref,
+    hold, answer, in_sem, key_sem, value_sem, answer_sem,
 ):
     resident = out_ref.shape[0] - query_ref.shape[0]
-    positions = codes_ref.shape[1]
-    tiles = pl.cdiv(positions, TILE)
+    tiles = codes_ref.shape[-3] // SPAN
     groups = 4
 
     def fetch(g, c):
-        part = pl.ds(c * TILE, min(TILE, positions - c * TILE))
-        return pltpu.make_async_copy(
-            codes_ref.at[0 if shared else g, part], hold.at[0 if shared else g, part], in_sem.at[0 if shared else g, c]
-        )
+        part = pl.ds(c * SPAN, SPAN)
+        return pltpu.make_async_copy(codes_ref.at[g, part], hold.at[g, part], in_sem.at[g, c])
 
     def put(g, c):
-        part = pl.ds(c * TILE, TILE)
+        part = pl.ds(c * SPAN, SPAN)
         slot = table_ref[first + 4 + g]
-        return pltpu.make_async_copy(
-            hold.at[0 if shared else g, part], arrived_ref.at[slot, part], code_sem.at[0 if shared else g, c]
+        chunks = hold.at[0 if shared else g, part]
+        target = arrived_ref.at[slot, part]
+        return (
+            pltpu.make_async_copy(chunks.at[:, pl.ds(0, CHUNK)], target.at[:, :, pl.ds(0, HEAD)], key_sem.at[g, c]),
+            pltpu.make_async_copy(
+                chunks.at[:, pl.ds(CHUNK, CHUNK)], target.at[:, :, pl.ds(HEAD, HEAD)], value_sem.at[g, c]
+            ),
         )
 
     def reply(g):
         slot = table_ref[first + 4 + g]
-        return pltpu.make_async_copy(
-            answer.at[0 if shared else g], out_ref.at[resident + slot], answer_sem.at[0 if shared else g]
-        )
-
-    for g in range(groups):
-        for c in range(tiles):
-
-            @pl.when(c * TILE < table_ref[first + g])
-            def _():
-                fetch(g, c).start()
-
-    ones = jnp.ones((HEAD, HEAD), jnp.bfloat16)
+        return pltpu.make_async_copy(answer.at[0 if shared else g], out_ref.at[resident + slot], answer_sem.at[g])
+
+    def inside(codes, left):
+        chunk = lax.broadcasted_iota(jnp.int32, codes.shape, 0)
+        row = lax.broadcasted_iota(jnp.int32, codes.shape, 1) & (CHUNK - 1)
+        return jnp.where(chunk * CHUNK + row < left, codes.astype(jnp.float32), 0.0).astype(jnp.bfloat16)
+
+    if not shared:
+        for g in range(groups):
+            for c in range(tiles):
+
+                @pl.when(c * TILE < table_ref[first + g])
+                def _():
+                    fetch(g, c).start()
+
+    def scaled(codes, factors, which):
+        wide = codes.astype(jnp.float32)
+        rows = []
+        for p in range(SPAN):
+            for k in range(CHUNK // BLOCK):
+                factor = factors[p, 2 * k + which : 2 * k + which + 1, :]
+                rows.append(wide[p, k * BLOCK : (k + 1) * BLOCK, :] * factor)
+        return jnp.concatenate(rows, axis=0).astype(jnp.bfloat16)
 
     def one_slot(g, carry):
         length = table_ref[first + g]
         slot = table_ref[first + 4 + g]
-        request = table_ref[first + 8 + g]
         at = 0 if shared else g
 
         @pl.when(length > 0)
         def _():
             rows = query_rows(query_ref[slot])
-            key_factor = factor_ref[pl.ds(2 * request, 1), :]
-            value_factor = factor_ref[pl.ds(2 * request + 1, 1), :]
 
             def tile(c, state):
-                for n in range(tiles):
-
-                    @pl.when(c == n)
+                part = pl.ds(pl.multiple_of(c * SPAN, SPAN), SPAN)
+                left = length - c * TILE
+                if shared:
+                    hold[0, part, :FACTORS, :] = inside(codes_ref[part, :FACTORS, :], left)
+                    factors = codes_ref[part, FACTORS:, :].astype(jnp.float32)
+                else:
+                    fetch(g, c).wait()
+
+                    @pl.when(left < TILE)
                     def _():
-                        fetch(g, n).wait()
-
-                part = pl.ds(pl.multiple_of(c * TILE, TILE), TILE)
-                left = length - c * TILE
-
-                @pl.when(left < TILE)
-                def _():
-                    codes = hold[at, part, :]
-                    place = lax.broadcasted_iota(jnp.int32, codes.shape, 0)
-                    hold[at, part, :] = jnp.where(place < left, codes.astype(jnp.float32), 0.0).astype(jnp.bfloat16)
-
-                put(g, c).start()
-                row = lax.broadcasted_iota(jnp.int32, (TILE, HEAD), 0)
-                column = lax.broadcasted_iota(jnp.int32, (TILE, HEAD), 1)
-                hit = column == row // BLOCK + c * (TILE // BLOCK)
-
-                def scaled(codes, factor):
-                    spread = jnp.where(hit, factor, 0.0).astype(jnp.bfloat16)
-                    wide = jnp.dot(spread, ones, preferred_element_type=jnp.float32)
-                    return (codes.astype(jnp.float32) * wide).astype(jnp.bfloat16)
-
-                keys = scaled(hold[at, part, :HEAD], key_factor)
-                values = scaled(hold[at, part, HEAD:], value_factor)
+                        hold[at, part, :FACTORS, :] = inside(hold[at, part, :FACTORS, :], left)
+
+                    factors = hold[at, part, FACTORS:, :].astype(jnp.float32)
+                for copy in put(g, c):
+                    copy.start()
+                keys = scaled(hold[at, part, :CHUNK, :], factors, 0)
+                values = scaled(hold[at, part, CHUNK:FACTORS, :], factors, 1)
                 return extend_row(state, rows, keys, values, left)
 
             state = lax.fori_loop(0, (length + TILE - 1) // TILE, tile, open_row(rows, fresh_ref[slot]))
@@ -369,16 +399,18 @@
 
             @pl.when(c * TILE < table_ref[first + g])
             def _():
-                put(g, c).wait()
-
-
-def fill_slots(first, shared, table, factors, queries, fresh, codes, out, arrived):
+                for copy in put(g, c):
+                    copy.wait()
+
+
+def fill_slots(first, shared, table, queries, fresh, codes, out, arrived):
     smem = pl.BlockSpec(memory_space=pltpu.SMEM)
     vmem = pl.BlockSpec(memory_space=pltpu.VMEM)
     hbm = pl.BlockSpec(memory_space=pltpu.HBM)
     slots = arrived.shape[0]
-    entries, tiles = codes.shape[0], pl.cdiv(codes.shape[1], TILE)
+    entries, chunks = 1 if shared else codes.shape[0], codes.shape[-3]
     tail = lambda width: pl.BlockSpec((slots, STEPS, width), lambda n: (1, 0, 0))
+    rows = FACTORS if shared else CHUNK_ROWS
     return pl.pallas_call(
         functools.partial(slot_kernel, first, shared),
         grid=(1,),
@@ -386,20 +418,21 @@
             jax.ShapeDtypeStruct(out.shape, out.dtype),
             jax.ShapeDtypeStruct(arrived.shape, arrived.dtype),
         ),
-        in_specs=[smem, vmem, tail(queries.shape[-1]), tail(2 * HEAD), hbm, hbm, hbm],
+        in_specs=[smem, tail(queries.shape[-1]), tail(2 * HEAD), vmem if shared else hbm, hbm, hbm],
         out_specs=(hbm, hbm),
-        input_output_aliases={5: 0, 6: 1},
+        input_output_aliases={4: 0, 5: 1},
         scratch_shapes=[
-            pltpu.VMEM((entries, tiles * TILE, 2 * HEAD), jnp.bfloat16),
+            pltpu.VMEM((entries, chunks, rows, HEAD), jnp.bfloat16),
             pltpu.VMEM((entries, STEPS, queries.shape[-1]), jnp.bfloat16),
-            pltpu.SemaphoreType.DMA((entries, tiles)),
-            pltpu.SemaphoreType.DMA((entries, tiles)),
-            pltpu.SemaphoreType.DMA((entries,)),
+            pltpu.SemaphoreType.DMA((4, chunks // SPAN)),
+            pltpu.SemaphoreType.DMA((4, chunks // SPAN)),
+            pltpu.SemaphoreType.DMA((4, chunks // SPAN)),
+            pltpu.SemaphoreType.DMA((4,)),
         ],
         compiler_params=pltpu.CompilerParams(vmem_limit_bytes=VMEM),
         cost_estimate=pl.CostEstimate(flops=1 << 30, bytes_accessed=8 << 20, transcendentals=1 << 20),
         name="moved_slots" if first == MOVED_LEN else "kept_slots",
-    )(table, factors, queries, fresh, codes, out, arrived)
+    )(table, queries, fresh, codes, out, arrived)
 
 
 def leave_kernel(shift, table_ref, codes_ref, out_ref, sem):
@@ -412,7 +445,7 @@
 def leave(shift, size, table, codes):
     return pl.pallas_call(
         functools.partial(leave_kernel, shift),
-        out_shape=jax.ShapeDtypeStruct((size, codes.shape[2]), codes.dtype),
+        out_shape=jax.ShapeDtypeStruct((size // CHUNK,) + codes.shape[2:], codes.dtype),
         in_specs=[pl.BlockSpec(memory_space=pltpu.SMEM), pl.BlockSpec(memory_space=pl.ANY)],
         out_specs=pl.BlockSpec(memory_space=pltpu.VMEM),
         scratch_shapes=[pltpu.SemaphoreType.DMA],
@@ -444,36 +477,30 @@
     positions = 32 * 4 * block_len
     query_view, fresh_view = queries[0, :, 0], new_kv[0, :, 0]
 
-    packed, table = pack(me, dest_group.transpose(0, 2, 1), prompt_len, block_table, pool)
+    scales = block_scales.reshape(16, layers * heads, 1, 2).transpose(1, 2, 3, 0)
+    scales = jnp.broadcast_to(scales, (layers * heads, 4, 2, 16)).reshape(layers * heads * 8, 16)
+    packed, table = pack(me, dest_group.transpose(0, 2, 1), prompt_len, block_table, scales, pool)
     landed = lax.all_to_all(
-        packed.reshape(128, 4 * block_len, width), everywhere, split_axis=0, concat_axis=0, tiled=True
-    ).reshape(4, positions, width)
-
-    out, arrived, taken = resident(res_len, table, query_view, fresh_view, res_cache[0, :, 0], slots, positions)
-
-    taken = (jnp.arange(16)[:, None] == taken[None, :]).astype(jnp.bfloat16)
-    scales = block_scales.reshape(16, layers * heads, 2).transpose(1, 2, 0).reshape(64, 16)
-    scales = jnp.dot(scales, taken, preferred_element_type=jnp.float32).astype(jnp.bfloat16)
-    scales = jnp.tile(scales.reshape(1, 32, 32), (4, 1, 1)).reshape(128, 32)
-    scales = lax.all_to_all(scales, everywhere, split_axis=0, concat_axis=0, tiled=True)
-    factors = scales.reshape(4, 32, 2, 4, 4).transpose(0, 3, 2, 1, 4).reshape(32, 128).astype(jnp.float32)
+        packed.reshape(128, CHUNK_ROWS, HEAD), everywhere, split_axis=0, concat_axis=0, tiled=True
+    ).reshape(4, 32, CHUNK_ROWS, HEAD)
+    out, arrived = resident(res_len, table, query_view, fresh_view, res_cache[0, :, 0], slots, positions)
 
     def kept(landed, out, arrived):
-        return fill_slots(KEPT_LEN, False, table, factors, query_view, fresh_view, landed, out, arrived)
+        return fill_slots(KEPT_LEN, False, table, query_view, fresh_view, landed, out, arrived)
 
     def moved(shared, codes, out, arrived):
-        return fill_slots(MOVED_LEN, shared, table, factors, query_view, fresh_view, codes, out, arrived)
+        return fill_slots(MOVED_LEN, shared, table, query_view, fresh_view, codes, out, arrived)
 
     def general(landed, out, arrived):
         codes = jnp.zeros_like(landed)
         for shift in range(1, 4):
             hit = table[MOVED_SHIFT : MOVED_SHIFT + 4] == shift
-            codes = jnp.where(hit[:, None, None], shifted(landed, shift), codes)
+            codes = jnp.where(hit[:, None, None, None], shifted(landed, shift), codes)
         out, arrived = kept(landed, out, arrived)
         return moved(False, codes, out, arrived)
 
     def direct(shift, size, landed, out, arrived):
-        codes = shifted(leave(shift, size, table, landed), shift)[None]
+        codes = shifted(leave(shift, size, table, landed), shift)
         out, arrived = kept(landed, out, arrived)
         return moved(True, codes, out, arrived)
 
@@ -481,7 +508,7 @@
         functools.partial(direct, shift, size) for shift in range(1, 4) for size in SIZES
     ]
     out, arrived = lax.switch(table[BRANCH], branches, landed, out, arrived)
-    return out[None, :, None], arrived[None, :, None]
+    return out[None, :, None], arrived.reshape(slots, positions, width)[None, :, None]
 
 
 def solution(mesh):

time: 128 us -> 95.3 us (0.74)
  blocking collectives: 20.7 us -> 0 us
  waiting for transfers between devices: 51.3 us -> 38.1 us
  starting transfers between devices: 7.62 us -> 12.6 us
  Pallas kernels: 41.8 us -> 39.1 us
    all_to_all x1 -> x0, blocking collectives: 20.7 us -> none  [on_device(): lax.all_to_all(scales, everywhere, split_axis=0, concat_axis=0, tiled=True)]
    all_to_all x1, waiting for transfers between devices: 50.8 us -> 33.2 us  [on_device(): lax.all_to_all(packed.reshape(128, CHUNK_ROWS, HEAD), everywhere, split_a...]
    all_to_all x1, starting transfers between devices: 5.82 us -> 11.6 us  [on_device(): lax.all_to_all(packed.reshape(128, CHUNK_ROWS, HEAD), everywhere, split_a...]
    ppermute x1, waiting for transfers between devices: 0.53 us -> 4.97 us  [shifted(): return lax.ppermute(values, 'src', [(g, (g + shift) % 4) for g in range(4)])]
    pallas_call x2, Pallas kernels: 12.5 us -> 9.95 us  [fill_slots(): pl.pallas_call(functools.partial(slot_kernel, first, shared), grid=(1,),...]
    broadcast_in_dim x0 -> x1, local copies, waits for them, and re-layouts: none -> 1.44 us  [on_device(): jnp.broadcast_to(scales, (layers * heads, 4, 2, 16))]
  transfers between devices with their start and end apart: 2 -> 2, of which waited for: 2 -> 2; matrix products, arithmetic and copies ran while one was open for 2% -> 1% of each run, Pallas kernels for 9% -> 31%
where the time goes in v3:
time: 95.3 us; the launch traced here: 94.9 us
  Pallas kernels  39.1 us (41%)
  waiting for transfers between devices  38.1 us (40%)
  starting transfers between devices  12.6 us (13%)
  local copies, waits for them, and re-layouts  3.65 us (4%)
  between operations  1.36 us (1%)
    all_to_all x1, waiting for transfers between devices, on_device(): lax.all_to_all(packed.reshape(128, CHUNK_ROWS, HEAD), everywhere, split_a...  33.2 us
    pallas_call x1, Pallas kernels, resident(): pl.pallas_call(resident_kernel, out_shape=(jax.ShapeDtypeStruct(queries.s...  20.7 us
    all_to_all x1, starting transfers between devices, on_device(): lax.all_to_all(packed.reshape(128, CHUNK_ROWS, HEAD), everywhere, split_a...  11.6 us
    pallas_call x2, Pallas kernels, fill_slots(): pl.pallas_call(functools.partial(slot_kernel, first, shared), grid=(1,),...  9.95 us
    pallas_call x1, Pallas kernels, pack(): pl.pallas_call(pack_kernel, out_shape=(jax.ShapeDtypeStruct((4, 32, CHUNK...  5.93 us
    ppermute x1, waiting for transfers between devices, shifted(): return lax.ppermute(values, 'src', [(g, (g + shift) % 4) for g in range(4)])  4.97 us
    pallas_call x1, Pallas kernels, leave(): pl.pallas_call(functools.partial(leave_kernel, shift), out_shape=jax.Shap...  2.44 us
  transfers between devices with their start and end apart: 2, of which 2 were waited for; matrix products, arithmetic and copies ran while one was open for 1% of the time, Pallas kernels for 31%

profile of v3, /device:TPU:0, one launch (start us, length us, event | category | flops | bytes accessed | tf_op | source)
XLA Modules:
  0.0 94.9 jit_solution(12040358259551091439)
XLA Ops:
  0.6 0.0 copy-start.2
  0.6 0.0 copy-start
  0.7 1.4 %broadcast_in_dim.69 = bf16[32,4,2,16]{3,2,1,0:T(2,128)(2,1)} broadcast(bf16[32,2,16]{2,1,0:T(2,128)(2,1)} %bitcast.65), dimensions={0,2,3} | broadcast | bytes 10240 | tf_op jit(solution)/shard_map/broadcast_in_dim | solution.py:481
  2.1 5.9 %pack.1 = (bf16[4,32,136,128]{3,2,1,0:T(8,128)(2,1)}, s32[32]{0:T(128)S(1)}) custom-call(s32[1]{0:T(128)} %bitcast.13.me_ref, s32[4,1,4]{2,1,0:T(1,128)} %bitcast.66, s32[4,4]{1,0:T(4,128)} %len_ref.2, s32[1,1,1,16]{3,2,1,0:T(1,128)} %block_ref.1, bf16[256,16]{1,0:T(8,128)(2,1)} %bitcast.64, bf16[16,32,16,256]{3,2,1,0:T(8,128)(2,1)} %bitcast.63), custom_call_target="tpu_custom_call" | custom-call | bytes 8388608 | tf_op jit(solution)/shard_map/pack/pallas_call | solution.py:172
  8.0 11.6 %all-to-all-start = ((bf16[128,136,128]{2,1,0:T(8,128)(2,1)}), bf16[128,136,128]{2,1,0:T(8,128)(2,1)}, u32[]{:S(2)}, u32[]{:S(2)}) async-start(bf16[128,136,128]{2,1,0:T(8,128)(2,1)} %bitcast.62), calls=%async_computation | async-start | bytes 8912896 | tf_op jit(solution)/shard_map/all_to_all | solution.py:483
  19.7 0.6 slice.8
  20.9 0.0 copy-done.2
  20.9 0.0 copy-done
  20.9 20.7 %resident.1 = (bf16[16,8,2048]{2,1,0:T(8,128)(2,1)S(1)}, bf16[8,32,64,256]{3,2,1,0:T(8,128)(2,1)}) custom-call(s32[1,8]{1,0:T(1,128)} %len_ref.3, s32[32]{0:T(128)S(1)} %get-tuple-element.333.table_ref, bf16[16,8,2048]{2,1,0:T(8,128)(2,1)S(1)} %bitcast.32, bf16[16,8,256]{2,1,0:T(8,128)(2,1)S(1)} %bitcast.47, bf16[8,3072,256]{2,1,0:T(8,128)(2,1)} %bitcast.61), custom_call_target="tpu_custom_call" | custom-call | flops 2147483648 | bytes 20971520 | tf_op jit(solution)/shard_map/resident/pallas_call | solution.py:286
  41.6 33.2 %all-to-all-done = bf16[128,136,128]{2,1,0:T(8,128)(2,1)} async-done(((bf16[128,136,128]{2,1,0:T(8,128)(2,1)}), bf16[128,136,128]{2,1,0:T(8,128)(2,1)}, u32[]{:S(2)}, u32[]{:S(2)}) %all-to-all-start) | async-done | bytes 4456480 | tf_op jit(solution)/shard_map/all_to_all | solution.py:483
  74.8 19.3 %conditional.1 = ((bf16[16,8,2048]{2,1,0:T(8,128)(2,1)S(1)}, bf16[8,32,64,256]{3,2,1,0:T(8,128)(2,1)})) conditional(s32[]{:T(128)} %bitcast.21, (s32[32]{0:T(128)S(1)}, bf16[128,136,128]{2,1,0:T(8,128)(2,1)}, bf16[16,8,2048]{2,1,0:T(8,128)(2,1)S(1)}, bf16[16,8,256]{2,1,0:T(8,128)(2,1)S(1)}, ...), branch_computations={%region_0.1_spmd, %region_1.2_spmd, %region_2.3_spmd, %region_3.4_... | conditional | flops 2154168320 | bytes 88080552 | solution.py:510
  74.8 2.4 %leave.21 = bf16[16,136,128]{2,1,0:T(8,128)(2,1)} custom-call(s32[32]{0:T(128)S(1)} %get-tuple-element.297.table_ref, bf16[4,32,136,128]{3,2,1,0:T(8,128)(2,1)} %bitcast.10.codes_ref), custom_call_target="tpu_custom_call" | custom-call | tf_op jit(solution)/shard_map/cond/branch_10_fun/leave/pallas_call | solution.py:446
  77.3 1.0 %collective-permute-start.9 = (bf16[16,136,128]{2,1,0:T(8,128)(2,1)}, bf16[16,136,128]{2,1,0:T(8,128)(2,1)S(1)}, u32[]{:S(2)}, u32[]{:S(2)}) collective-permute-start(bf16[16,136,128]{2,1,0:T(8,128)(2,1)} %leave.21), channel_id=1, source_target_pairs={{0,3},{1,0},{2,1},{3,2},{4,7},{5,4},{6,5},{7,6},{8,11},{9,8},{10,9... | collective-permute-start | bytes 1671176 | tf_op jit(solution)/shard_map/cond/branch_10_fun/ppermute | solution.py:458
  78.3 8.5 %kept_slots.23 = (bf16[16,8,2048]{2,1,0:T(8,128)(2,1)S(1)}, bf16[8,32,64,256]{3,2,1,0:T(8,128)(2,1)}) custom-call(s32[32]{0:T(128)S(1)} %get-tuple-element.297.table_ref, bf16[16,8,2048]{2,1,0:T(8,128)(2,1)S(1)} %get-tuple-element.298.query_ref, bf16[16,8,256]{2,1,0:T(8,128)(2,1)S(1)} %get-tuple-element.299.fresh_ref, ...), custom_call_target="tpu_custom_call", output_to_operand_aliasing={{0}: (4, {}), {1}: (5, {})} | custom-call | flops 1073741824 | bytes 8388608 | tf_op jit(solution)/shard_map/cond/branch_10_fun/kept_slots/pallas_call | solution.py:414
  86.8 5.0 %collective-permute-done.9.codes_ref = bf16[16,136,128]{2,1,0:T(8,128)(2,1)S(1)} collective-permute-done((bf16[16,136,128]{2,1,0:T(8,128)(2,1)}, bf16[16,136,128]{2,1,0:T(8,128)(2,1)S(1)}, u32[]{:S(2)}, u32[]{:S(2)}) %collective-permute-start.9) | collective-permute-done | bytes 557088 | tf_op jit(solution)/shard_map/cond/branch_10_fun/ppermute | solution.py:458
  91.8 0.0 copy-start.11
  91.8 0.8 copy-done.11
  92.6 1.4 %moved_slots.23 = (bf16[16,8,2048]{2,1,0:T(8,128)(2,1)S(1)}, bf16[8,32,64,256]{3,2,1,0:T(8,128)(2,1)}) custom-call(s32[32]{0:T(128)S(1)} %get-tuple-element.297.table_ref, bf16[16,8,2048]{2,1,0:T(8,128)(2,1)S(1)} %get-tuple-element.298.query_ref, bf16[16,8,256]{2,1,0:T(8,128)(2,1)S(1)} %get-tuple-element.299.fresh_ref, ...), custom_call_target="tpu_custom_call", output_to_operand_aliasing={{0}: (4, {}), {1}: (5, {})} | custom-call | flops 1073741824 | bytes 8388608 | tf_op jit(solution)/shard_map/cond/branch_10_fun/moved_slots/pallas_call | solution.py:414
  94.1 0.0 copy-start.1
  94.1 0.8 copy-done.1
Async XLA Ops:
  0.6 20.3 %copy-start.2 = (bf16[1,16,1,8,256]{4,3,2,1,0:T(8,128)(2,1)S(1)}, bf16[1,16,1,8,256]{4,3,2,1,0:T(8,128)(2,1)}, u32[]{:S(2)}) copy-start(bf16[1,16,1,8,256]{4,3,2,1,0:T(8,128)(2,1)} %param.30) | copy-start | bytes 196612
  0.6 20.3 %copy-start = (bf16[1,16,1,8,2048]{4,3,2,1,0:T(8,128)(2,1)S(1)}, bf16[1,16,1,8,2048]{4,3,2,1,0:T(8,128)(2,1)}, u32[]{:S(2)}) copy-start(bf16[1,16,1,8,2048]{4,3,2,1,0:T(8,128)(2,1)} %param.29) | copy-start | bytes 1572868
  8.0 66.8 %all-to-all-start = ((bf16[128,136,128]{2,1,0:T(8,128)(2,1)}), bf16[128,136,128]{2,1,0:T(8,128)(2,1)}, u32[]{:S(2)}, u32[]{:S(2)}) async-start(bf16[128,136,128]{2,1,0:T(8,128)(2,1)} %bitcast.62), calls=%async_computation | async-start | bytes 8912896 | tf_op jit(solution)/shard_map/all_to_all | solution.py:483
  77.3 14.5 %collective-permute-start.9 = (bf16[16,136,128]{2,1,0:T(8,128)(2,1)}, bf16[16,136,128]{2,1,0:T(8,128)(2,1)S(1)}, u32[]{:S(2)}, u32[]{:S(2)}) collective-permute-start(bf16[16,136,128]{2,1,0:T(8,128)(2,1)} %leave.21), channel_id=1, source_target_pairs={{0,3},{1,0},{2,1},{3,2},{4,7},{5,4},{6,5},{7,6},{8,11},{9,8},{10,9... | collective-permute-start | bytes 1671176 | tf_op jit(solution)/shard_map/cond/branch_10_fun/ppermute | solution.py:458
  91.8 0.8 copy-start.11
  94.1 0.8 copy-start.1
